TPU v7x, 512 devices: a whole 4x8x8 slice. The times are simulated.
512 devices in a mesh: dp: 32 (over y_hi, z, core), seq: 16 (over x, y_lo).
Axes of the slice: x: 4, y: 8 (y_hi: 2, y_lo: 4; y = y_hi * 4 + y_lo), z: 8, core: 2. Of those that a mesh axis runs over, the one named last changes fastest.
Arguments:
- out_grad: bfloat16 [32, 4096, 2240], P('dp', 'seq'), may hold values from -384 to 384
- out_weight: bfloat16 [1120, 2240], P('dp'), may hold values from -0.1875 to 0.1875
- queries: bfloat16 [32, 4096, 1120], P('dp', 'seq'), may hold values from -6 to 6
- keys: bfloat16 [32, 4096, 1120], P('dp', 'seq'), may hold values from -6 to 6
- values: bfloat16 [32, 4096, 1120], P('dp', 'seq'), may hold values from -6 to 6
- query_gain: float32 [1120], P('dp'), may hold values from 0.1 to 1.9
- key_norm_gain: float32 [1120], P('dp'), may hold values from 0.1 to 1.9
Outputs:
- query_grad: bfloat16 [32, 4096, 1120], P('dp', 'seq')
- key_gradient: bfloat16 [32, 4096, 1120], P('dp', 'seq')
- value_grad: bfloat16 [32, 4096, 1120], P('dp', 'seq')
- query_gain_grad: float32 [1120], P('dp')
- key_gain_grad: float32 [1120], P('dp')
All inputs are finite; a program needn't handle non-finite values.
Results may differ from a plain program's by a relative error of at most 0.0085.
Values may be sent and summed in bfloat16 or wider, within the bound.
A program may use at most 64 MiB of HBM per device.

v0:
```python
import jax
import jax.numpy as jnp
from jax import lax
from jax.sharding import PartitionSpec as P

HEADS = 10
HEAD = 112


HIGH = lax.Precision.HIGHEST


def normalized_rows(raw, gain):
    rows = raw.shape[0]
    flat = raw.astype(jnp.float32).reshape(rows, HEADS, HEAD)
    scale = lax.rsqrt(jnp.mean(flat * flat, axis=2, keepdims=True) + 1e-06)
    return (flat, scale, gain.reshape(HEADS, HEAD)[None] * flat * scale)


def norm_backward(flat, scale, gain, grad):
    shaped = gain.reshape(HEADS, HEAD)[None] * grad
    inner = jnp.mean(shaped * flat, axis=2, keepdims=True)
    return (scale * shaped - flat * scale**3 * inner, jnp.sum(grad * flat * scale, axis=0))


def local(out_grad, out_weight, queries, keys, values, query_gain, key_norm_gain):
    rows = queries.shape[1]
    tokens_all = rows * lax.axis_size("seq")
    width = HEADS * HEAD
    full_qgain, complete_key_gain = (
        lax.all_gather(query_gain, "dp", axis=0, tiled=True),
        lax.all_gather(key_norm_gain, "dp", axis=0, tiled=True),
    )
    qflat, qscale, qnorm = normalized_rows(queries[0], full_qgain)
    flattened_keys, key_inverse_scale, key_rms_norm = normalized_rows(keys[0], complete_key_gain)
    phi_q = jnp.maximum(qnorm, 0.0).astype(jnp.bfloat16).astype(jnp.float32)
    phi_k = jnp.maximum(key_rms_norm, 0.0).astype(jnp.bfloat16).astype(jnp.float32)
    vals = values[0].astype(jnp.float32).reshape(rows, HEADS, HEAD)
    local_summary = jnp.einsum("thi,thj->hij", phi_k, vals, precision=HIGH)
    local_total = jnp.sum(phi_k, axis=0)
    grad_rows = out_grad[0]
    attn_grad = lax.dot_general(
        grad_rows,
        lax.all_gather(out_weight, "dp", axis=0, tiled=True),
        (((1,), (1,)), ((), ())),
        preferred_element_type=jnp.float32,
    ).astype(jnp.bfloat16)
    attn_grad = attn_grad.astype(jnp.float32).reshape(rows, HEADS, HEAD)
    summary, total = lax.psum((local_summary, local_total), "seq")
    denom = jnp.einsum("thi,hi->th", phi_q, total, precision=HIGH)[:, :, None] + tokens_all * 1.0
    attended = jnp.einsum("thi,hij->thj", phi_q, summary, precision=HIGH) / denom
    num_grad = attn_grad / denom
    denom_grad = -jnp.sum(attn_grad * attended, axis=2, keepdims=True) / denom
    local_sgrad = jnp.einsum("thi,thj->hij", phi_q, num_grad, precision=HIGH)
    local_tgrad = jnp.sum(denom_grad * phi_q, axis=0)
    summary_grad, total_grad = lax.psum((local_sgrad, local_tgrad), "seq")
    phi_q_grad = (
        jnp.einsum("thj,hij->thi", num_grad, summary, precision=HIGH) + denom_grad * total[None]
    )
    phi_k_grad = jnp.einsum("thj,hij->thi", vals, summary_grad, precision=HIGH) + total_grad[None]
    value_grad = jnp.einsum("thi,hij->thj", phi_k, summary_grad, precision=HIGH)
    nq_grad = jnp.where(qflat > 0, phi_q_grad, 0.0)
    normed_key_gradient = jnp.where(flattened_keys > 0, phi_k_grad, 0.0)
    query_grad, query_part = norm_backward(qflat, qscale, full_qgain, nq_grad)
    key_gradient, key_portion = norm_backward(
        flattened_keys, key_inverse_scale, complete_key_gain, normed_key_gradient
    )
    query_part = query_part.reshape(width)
    key_portion = key_portion.reshape(width)
    summed_q, summed_k = lax.psum((query_part, key_portion), "seq")
    gain_q_out, gain_k_out = (
        lax.psum_scatter(summed_q, "dp", scatter_dimension=0, tiled=True),
        lax.psum_scatter(summed_k, "dp", scatter_dimension=0, tiled=True),
    )
    return (
        query_grad.reshape(1, rows, width).astype(jnp.bfloat16),
        key_gradient.reshape(1, rows, width).astype(jnp.bfloat16),
        value_grad.reshape(1, rows, width).astype(jnp.bfloat16),
        gain_q_out,
        gain_k_out,
    )


def solution(mesh):
    placed = (
        P("dp", "seq", None),
        P("dp", None),
        P("dp", "seq", None),
        P("dp", "seq", None),
        P("dp", "seq", None),
        P("dp"),
        P("dp"),
    )
    return jax.shard_map(
        local,
        mesh=mesh,
        in_specs=placed,
        out_specs=(
            P("dp", "seq", None),
            P("dp", "seq", None),
            P("dp", "seq", None),
            P("dp"),
            P("dp"),
        ),
        check_vma=False,
    )
```

profile of v0, /device:TPU:8, one launch (start us, length us, event | category | flops | bytes accessed | tf_op | source)
XLA Modules:
  0.0 697.8 jit_solution(16011148427439019696)
XLA Ops:
  7.2 0.0 copy-start
  7.2 0.0 copy-start.3
  7.2 0.0 all-gather.3.cloned.1.call-start
  7.2 0.7 all-gather.3.cloned.1.call-update
  7.9 0.0 all-reduce.10.cloned.1.call-start
  8.0 1.4 fusion.20
  10.0 0.9 dynamic-update-slice.1
  10.9 0.9 dynamic-update-slice
  11.7 181.9 %all-reduce.5 = (f32[1120]{0:T(1024)S(1)}, f32[1120]{0:T(1024)S(1)}) all-reduce(f32[1120]{0:T(1024)S(1)} %dynamic-update-slice.1, f32[1120]{0:T(1024)S(1)} %dynamic-update-slice), channel_id=1, replica_groups=mesh['dp'=32,'seq'=16] {'dp'}, use_global_device_ids=true, to_apply=%add.1 | all-reduce | flops 2240 | bytes 17920
  193.6 0.1 mul.179
  193.6 0.1 mul.177
  193.7 1.2 multiply_reduce_fusion.5
  195.0 0.3 fusion.9
  195.2 0.2 convert_reduce_fusion
  195.5 0.1 reduce_sum.88
  195.6 42.7 %psum.43 = f32[10,112]{1,0:T(8,128)S(1)} all-reduce(f32[10,112]{1,0:T(8,128)S(1)} %reduce_sum.88), channel_id=1, replica_groups=mesh['dp'=32,'seq'=16] {'seq'}, use_global_device_ids=true, to_apply=%region_4.0 | all-reduce | flops 1120 | bytes 8960 | tf_op jit(solution)/shard_map/psum | solution.py:49
  238.2 1.2 multiply_reduce_fusion.6
  239.5 0.2 maximum_convert_fusion
  239.7 0.8 copy-done.4
  240.5 0.3 fusion.16
  240.9 0.6 fusion.15
  241.5 1.2 fusion.14
  242.7 6.8 reshape.152
  249.4 4.0 convolution_convert_fusion
  253.5 0.8 copy-done.13
  254.3 1.6 fusion.11
  255.9 0.0 all-reduce.10.cloned.1.call-update
  255.9 2.1 fusion.7
  258.7 159.5 %all-reduce.10.cloned.1.call-done = (f32[10,112,112]{2,1,0:T(8,128)}, f32[10,112,112]{2,1,0:T(8,128)}) async-done(((f32[10,112,112]{2,1,0:T(8,128)}, f32[10,112,112]{2,1,0:T(8,128)}), (f32[10,112,112]{2,1,0:T(8,128)}, f32[10,112,112]{2,1,0:T(8,128)})) %all-reduce.10.cloned.1.call-update) | async-done | bytes 1003536 | tf_op jit(solution)/shard_map/psum | solution.py:49
  418.2 2.2 fusion.5
  420.5 3.1 multiply_reduce_fusion.1
  423.6 0.7 reshape.139
  424.3 0.7 broadcast_multiply_fusion.1
  425.0 2.7 convolution_convert_fusion.1
  427.8 0.1 mul.192
  427.9 1.0 copy-done.6
  428.8 0.2 multiply_reduce_fusion.3
  429.1 0.7 reduce_sum.92
  429.7 39.2 %psum.45 = f32[10,112]{1,0:T(8,128)S(1)} all-reduce(f32[10,112]{1,0:T(8,128)} %reduce_sum.92), channel_id=1, replica_groups=mesh['dp'=32,'seq'=16] {'seq'}, use_global_device_ids=true, to_apply=%region_9.10 | all-reduce | flops 1120 | bytes 8960 | tf_op jit(solution)/shard_map/psum | solution.py:56
  469.0 3.8 multiply_reduce_fusion
  472.8 0.8 reshape.140
  473.5 166.9 %all-reduce.4 = (f32[1120]{0:T(1024)}, f32[1120]{0:T(1024)}) all-reduce(f32[1120]{0:T(1024)} %reshape.139, f32[1120]{0:T(1024)S(1)} %reshape.140), channel_id=2, replica_groups=mesh['dp'=32,'seq'=16] {'dp'}, use_global_device_ids=true, to_apply=%region_13.14.clone | all-reduce | flops 2240 | bytes 17920
  640.5 0.8 dynamic-slice.3
  641.2 0.8 dynamic-slice.5
  642.0 1.3 broadcast_multiply_fusion
  643.3 44.0 %all-reduce.6 = (f32[35]{0:T(128)}, f32[35]{0:T(128)}) all-reduce(f32[35]{0:T(128)S(1)} %dynamic-slice.3, f32[35]{0:T(128)S(1)} %dynamic-slice.5), channel_id=1, replica_groups=mesh['dp'=32,'seq'=16] {'seq'}, use_global_device_ids=true, to_apply=%region_12.13 | all-reduce | flops 70 | bytes 560 | tf_op jit(solution)/shard_map/psum | solution.py:70
  687.3 2.5 subtract_convert_fusion.1
  689.8 1.1 subtract_convert_fusion
  (31 shorter events, 0.1 us)
Async XLA Ops:
  7.2 242.2 %copy-start = (bf16[1,256,2240]{1,2,0:T(8,128)(2,1)S(1)}, bf16[1,256,2240]{1,2,0:T(8,128)(2,1)}, u32[]{:S(2)}) copy-start(bf16[1,256,2240]{1,2,0:T(8,128)(2,1)} %param.7) | copy-start | bytes 3440644
  7.2 187.8 %copy-start.3 = (bf16[1,256,1120]{1,2,0:T(8,128)(2,1)S(1)}, bf16[1,256,1120]{1,2,0:T(8,128)(2,1)}, u32[]{:S(2)}) copy-start(bf16[1,256,1120]{1,2,0:T(8,128)(2,1)} %param.10) | copy-start | bytes 1720324
  7.2 235.5 %all-gather.3.cloned.1.call-start = ((), (), s32[]{:S(2)}) async-start(), calls=%async_computation | async-start | bytes 6082560 | tf_op jit(solution)/shard_map/all_gather | solution.py:44
  7.9 410.3 %all-reduce.10.cloned.1.call-start = ((), (), s32[]{:S(2)}) async-start(), calls=%async_computation.1 | async-start | bytes 2293760 | tf_op jit(solution)/shard_map/psum | solution.py:49
  239.5 2.0 copy-start.2
  239.7 0.8 copy-start.4
  249.4 4.9 copy-start.5
  249.4 4.9 copy-start.10
  253.5 0.8 copy-start.13
  418.2 2.3 copy-start.11
  418.2 2.3 copy-start.12
  418.2 2.3 copy-start.14
  420.5 3.1 copy-start.8
  425.0 2.7 copy-start.9
  427.8 1.1 copy-start.6
  687.3 2.5 copy-start.1
  687.3 2.5 copy-start.7
Sparse Core Ops, SparseCore 0:
  11.3 122.7 all-gather.2
  256.0 162.1 all-reduce.9
where the time goes:
time: 699 us; the launch traced here: 698 us
  blocking collectives  475 us (68%)
  waiting for transfers between devices  160 us (23%)
  matrix products  19 us (3%)
  local copies, waits for them, and re-layouts  16.4 us (2%)
  between operations  15.6 us (2%)
  other arithmetic  11.8 us (2%)
    unnamed x2, blocking collectives  349 us
    psum x1, waiting for transfers between devices, local(): summary, total = lax.psum((local_summary, local_total), 'seq')  160 us
    psum x1, blocking collectives, local(): summed_q, summed_k = lax.psum((query_part, key_portion), 'seq')  44 us
    psum x1, blocking collectives, local(): summary, total = lax.psum((local_summary, local_total), 'seq')  42.7 us
    psum x1, blocking collectives, local(): summary_grad, total_grad = lax.psum((local_sgrad, local_tgrad), 'seq')  39.2 us
    unnamed x38, local copies, waits for them, and re-layouts  14 us
  transfers between devices with their start and end apart: 2, of which 1 were waited for; matrix products, arithmetic and copies ran while one was open for 2% of the time, Pallas kernels for 0%

commit v1 on v0

v1 whole, which is shorter than its diff:
```python
import functools

import jax
import jax.numpy as jnp
from jax import lax
from jax.experimental import pallas as pl
from jax.experimental.pallas import tpu as pltpu
from jax.sharding import PartitionSpec as P

HEADS = 10
HEAD = 112
PAD = 128
ROWS = 256
WIDTH = HEADS * HEAD
MODEL = 2240
TOKENS = 4096
SEQ = 16
DP = 32
OWN = 35
HALF = 1152
CUT = 640
WIN = 80
PIECE = 80
BF = jnp.bfloat16
F32 = jnp.float32
MESH = pl.DeviceIdType.MESH


def first_tile(j):
    return (35 * j) // 8


OWNER = [max(j for j in range(SEQ) if first_tile(j) <= t) for t in range(70)]


def iota(shape, axis):
    return lax.broadcasted_iota(jnp.int32, shape, axis)


def dot_nt(a, b):
    return lax.dot_general(a, b, (((1,), (1,)), ((), ())), preferred_element_type=F32)


def dot_tn(a, b):
    return lax.dot_general(a, b, (((0,), (0,)), ((), ())), preferred_element_type=F32)


def dot_nn(a, b):
    return lax.dot_general(a, b, (((1,), (0,)), ((), ())), preferred_element_type=F32)


def kernel(
    og_in, w_in, q_in, k_in, v_in, gq_in, gk_in,
    qg_out, kg_out, vg_out, gqg_out, gkg_out,
    k_raw, v_raw, q_raw, w_raw, og, og_sib,
    kh, qh, vx, rkb, rqb, kp, ngx, qs,
    wpk, pair, wbuf, wh, att, att_send, gains,
    s_loc, s_recv, s_all, s_full,
    g_loc, g_recv, g_all, g_full,
    win_send, win_recv,
    in_sem, misc_s, misc_r, pair_s, pair_r, z_s, z_r, x_s, x_r,
    s_rs_s, s_rs_r, s_ag_s, s_ag_r, g_rs_s, g_rs_r, g_ag_s, g_ag_r, r_s, r_r,
):
    d = lax.axis_index("dp")
    s = lax.axis_index("seq")
    y = d // 16
    z = (d // 2) % 8
    c = d % 2
    p = (s // 4) % 2
    sib = (y * 16 + z * 2 + (1 - c), s)

    def remote(src, dst, ss, rs, dev):
        return pltpu.make_async_remote_copy(
            src_ref=src, dst_ref=dst, send_sem=ss, recv_sem=rs,
            device_id=dev, device_id_type=MESH,
        )

    ins = [
        pltpu.make_async_copy(a, b, in_sem.at[i])
        for i, (a, b) in enumerate(
            ((w_in, w_raw), (k_in, k_raw), (v_in, v_raw), (q_in, q_raw), (og_in, og))
        )
    ]
    for cp in ins:
        cp.start()
    bar = pltpu.get_barrier_semaphore()

    def greet_seq(o, u):
        pl.semaphore_signal(bar, inc=1, device_id=(d, (s + o) % SEQ), device_id_type=MESH)
        return u

    def greet_dp(o, u):
        pl.semaphore_signal(bar, inc=1, device_id=((d + o) % DP, s), device_id_type=MESH)
        return u

    lax.fori_loop(1, SEQ, greet_seq, 0)
    lax.fori_loop(1, DP, greet_dp, 0)

    ins[0].wait()
    wpk[...] = jnp.zeros_like(wpk)
    wpk[0:OWN, 0:MODEL] = w_raw[...]
    diag = iota((48, OWN), 0) == iota((48, OWN), 1)
    lane = iota((48, 64), 1)
    extra = jnp.zeros((48, 64), F32)
    for n, ref in enumerate((gq_in, gk_in)):
        col = jnp.sum(jnp.where(diag, jnp.broadcast_to(ref[...], (48, OWN)), 0.0), axis=1, keepdims=True)
        rest = col
        for m in range(3):
            part = rest.astype(BF).astype(F32)
            extra = jnp.where(lane == 3 * n + m, part, extra)
            rest = rest - part
    wpk[:, MODEL:] = extra.astype(BF)

    pl.semaphore_wait(bar, SEQ - 1 + DP - 1)

    far = remote(wpk, pair.at[c], pair_s.at[0], pair_r.at[c], ((1 - y) * 16 + z * 2 + y, s))
    near = remote(wpk, pair.at[c], pair_s.at[1], pair_r.at[c], sib)
    far.start()

    @pl.when(c != y)
    def _():
        near.start()

    @pl.when(c == y)
    def _():
        pair[c] = wpk[...]

    og_copy = remote(og_in, og_sib, misc_s.at[0], misc_r.at[0], sib)
    og_copy.start()

    kh[...] = jnp.zeros_like(kh)
    qh[...] = jnp.zeros_like(qh)
    vx[...] = jnp.where(iota(vx.shape, 2) == HEAD, 1.0, 0.0).astype(BF)
    s_full[...] = jnp.zeros_like(s_full)
    g_full[...] = jnp.zeros_like(g_full)
    ins[1].wait()
    ins[2].wait()
    for h in range(HEADS):
        cols = pl.ds(HEAD * h, HEAD)
        kh[h, :, 0:HEAD] = k_raw[:, cols]
        vx[h, :, 0:HEAD] = v_raw[:, cols]
    for h in range(HEADS):
        kf = kh[h].astype(F32)
        r = lax.rsqrt(jnp.sum(kf * kf, axis=1, keepdims=True) * (1.0 / HEAD) + 1e-06)
        rb = jnp.broadcast_to(r, (ROWS, PAD))
        rkb[h] = rb
        phi = jnp.maximum(kf * rb, 0.0).astype(BF)
        kp[h] = phi
        summ = dot_tn(phi, vx[h])
        s_loc[HEAD * h : HEAD * (h + 1), :] = summ[0:HEAD].astype(BF)

    def rs_send(loc, recv, ss, rs):
        def step(o, u):
            j = (s + o) % SEQ
            rows = pl.ds(pl.multiple_of(first_tile(j) * 16, 16), PIECE)
            remote(loc.at[rows], recv.at[o], ss.at[o], rs.at[o], (d, j)).start()
            return u

        lax.fori_loop(1, SEQ, step, 0)

    def rs_sum(loc, recv, ss, rs):
        acc = loc[pl.ds(pl.multiple_of(first_tile(s) * 16, 16), PIECE), :].astype(F32)

        def step(o, acc):
            remote(loc.at[pl.ds(0, PIECE)], recv.at[o], ss.at[o], rs.at[o], (d, s)).wait_recv()
            return acc + recv[o].astype(F32)

        return lax.fori_loop(1, SEQ, step, acc)

    def ag_send(all_, acc, ss, rs):
        all_[s] = acc.astype(BF)

        def step(o, u):
            remote(all_.at[s], all_.at[s], ss.at[o], rs.at[o], (d, (s + o) % SEQ)).start()
            return u

        lax.fori_loop(1, SEQ, step, 0)

    def ag_wait(all_, full, ss, rs):
        def step(o, u):
            j = (s + SEQ - o) % SEQ
            remote(all_.at[j], all_.at[j], ss.at[o], rs.at[o], (d, j)).wait_recv()
            return u

        lax.fori_loop(1, SEQ, step, 0)
        for t in range(70):
            j = OWNER[t]
            k = 16 * (t - first_tile(j))
            full[t // 7, 16 * (t % 7) : 16 * (t % 7) + 16, :] = all_[j, k : k + 16, :]

    rs_send(s_loc, s_recv, s_rs_s, s_rs_r)

    pair_wait = [remote(wpk, pair.at[i], pair_s.at[0], pair_r.at[i], sib) for i in range(2)]

    @pl.when((c != y) | (c == 1))
    def _():
        pair_wait[0].wait_recv()

    @pl.when((c != y) | (c == 0))
    def _():
        pair_wait[1].wait_recv()

    m = iota((WIN, 96), 1)
    to = (70 * z) % 16 + jnp.where(m < 48, m, m - 13)
    to = jnp.where(to >= WIN, to - WIN, to)
    good = (m < OWN) | ((m >= 48) & (m < 48 + OWN))
    place = jnp.where((iota((WIN, 96), 0) == to) & good, 1.0, 0.0).astype(BF)
    both = pair[...].reshape(96, 2 * HALF)
    window = dot_nn(place, both).astype(BF)
    wbuf[0, z] = window[:, :HALF]
    wbuf[1, z] = window[:, HALF:]

    up = (y * 16 + ((z + 1) % 8) * 2 + c, s)
    down = (y * 16 + ((z + 7) % 8) * 2 + c, s)
    right = (d, (s + 4) % SEQ)
    left = (d, (s + 12) % SEQ)
    part_a = pl.ds(0, CUT)
    part_b = pl.ds(CUT, HALF - CUT)

    def z_copy(way, k):
        b = (z - (k - 1) + 8) % 8 if way == 0 else (z + (k - 1)) % 8
        ref = wbuf.at[p, b]
        if k == 4:
            ref = wbuf.at[p, b, :, part_a if way == 0 else part_b]
        return remote(ref, ref, z_s.at[way, k - 1], z_r.at[way, k - 1], up if way == 0 else down)

    def x_copy(way, rel):
        b = (z + rel) % 8
        ref = wbuf.at[p, b, :, part_a if way == 0 else part_b]
        return remote(ref, ref, x_s.at[way, rel - 1], x_r.at[way, rel - 1], right if way == 0 else left)

    def x_wait(way, rel):
        b = (z + rel) % 8
        ref = wbuf.at[1 - p, b, :, part_a if way == 0 else part_b]
        remote(ref, ref, x_s.at[way, rel - 1], x_r.at[way, rel - 1], right).wait_recv()

    def z_step(k):
        z_copy(0, k).wait_recv()
        if k < 4:
            z_copy(0, k + 1).start()
            x_copy(0, 8 - k).start()
            x_copy(1, 8 - k).start()
        else:
            x_copy(0, 4).start()
        z_copy(1, k).wait_recv()
        if k < 4:
            z_copy(1, k + 1).start()
            x_copy(0, k).start()
            x_copy(1, k).start()
        else:
            x_copy(1, 4).start()

    z_copy(0, 1).start()
    z_copy(1, 1).start()

    ins[3].wait()
    for h in range(HEADS):
        qh[h, :, 0:HEAD] = q_raw[:, HEAD * h : HEAD * (h + 1)]
    for h in range(HEADS):
        qf = qh[h].astype(F32)
        r = lax.rsqrt(jnp.sum(qf * qf, axis=1, keepdims=True) * (1.0 / HEAD) + 1e-06)
        rqb[h] = jnp.broadcast_to(r, (ROWS, PAD))

    z_step(1)
    ag_send(s_all, rs_sum(s_loc, s_recv, s_rs_s, s_rs_r), s_ag_s, s_ag_r)
    z_step(2)
    z_step(3)
    ag_wait(s_all, s_full, s_ag_s, s_ag_r)
    z_step(4)
    for k in (1, 2, 3):
        for rel in (8 - k, k):
            x_wait(0, rel)
            x_wait(1, rel)
    x_wait(0, 4)
    x_wait(1, 4)

    row = iota((16, HALF), 0)
    for t in range(35):
        out = pl.ds(PAD * (t // 7) + 16 * (t % 7), 16)
        for e in range(2):
            tile = None
            for b in range(8):
                phase = (70 * b) % 16
                k = t - (70 * b) // 16
                over = phase + 70 - WIN
                if 0 <= k < 5:
                    piece = wbuf[e, b, 16 * k : 16 * k + 16, :]
                    if over > 0 and k == 0:
                        piece = jnp.where(row >= phase, piece, jnp.zeros_like(piece))
                elif k == 5 and over > 0:
                    piece = wbuf[e, b, 0:16, :]
                    piece = jnp.where(row < over, piece, jnp.zeros_like(piece))
                else:
                    continue
                tile = piece if tile is None else tile + piece
            wh[out, HALF * e : HALF * (e + 1)] = tile
    for h in range(5):
        wh[PAD * h + HEAD : PAD * (h + 1), :] = jnp.zeros((PAD - HEAD, 2 * HALF), BF)

    og_copy.wait_recv()
    ins[4].wait()
    sel_row = iota((16, 128), 0)
    sel_lane = iota((16, 128), 1)
    pick = ((sel_row == 0) & (sel_lane >= 64) & (sel_lane < 67)) | (
        (sel_row == 8) & (sel_lane >= 67) & (sel_lane < 70)
    )
    gains[c] = dot_nt(jnp.where(pick, 1.0, 0.0).astype(BF), wh[:, 2 * HALF - 128 :])
    gain_copy = remote(gains.at[c], gains.at[c], misc_s.at[1], misc_r.at[1], sib)
    gain_copy.start()
    att_send[...] = dot_nt(og_sib[...], wh[:, 0:MODEL]).astype(BF)
    att_copy = remote(att_send, att.at[c], misc_s.at[2], misc_r.at[2], sib)
    att_copy.start()
    att[c] = dot_nt(og[...], wh[:, 0:MODEL]).astype(BF)
    remote(gains.at[1 - c], gains.at[1 - c], misc_s.at[1], misc_r.at[1], sib).wait_recv()
    remote(att_send, att.at[1 - c], misc_s.at[2], misc_r.at[2], sib).wait_recv()

    def gain(n, h):
        return gains[h // 5, 8 * n : 8 * n + 1, PAD * (h % 5) : PAD * (h % 5 + 1)]

    tl = iota((ROWS, PAD), 1)
    for h in range(HEADS):
        gqk = gain(0, h) * gain(1, h)
        phi = jnp.maximum(qh[h].astype(F32) * rqb[h], 0.0)
        num = dot_nn((phi * gqk).astype(BF), s_full[h])
        inv = 1.0 / (num[:, HEAD : HEAD + 1] + float(TOKENS))
        ag = att[h // 5, :, PAD * (h % 5) : PAD * (h % 5 + 1)].astype(F32)
        ng = ag * inv
        dg = -jnp.sum(ng * num, axis=1, keepdims=True) * inv
        nx = jnp.where(tl == HEAD, dg, ng).astype(BF)
        ngx[h] = nx
        g_loc[HEAD * h : HEAD * (h + 1), :] = dot_tn(phi.astype(BF), nx)[0:HEAD].astype(BF)

    rs_send(g_loc, g_recv, g_rs_s, g_rs_r)

    def norm_back(raw, rb, grad):
        f = raw.astype(F32)
        a = jnp.where(f > 0, grad, 0.0)
        hat = f * rb
        mean = jnp.sum(a * hat, axis=1, keepdims=True) * (1.0 / HEAD)
        return (rb * (a - hat * mean)).astype(BF)

    for h in range(HEADS):
        gqk = gain(0, h) * gain(1, h)
        g = dot_nt(ngx[h], s_full[h]) * gqk
        qg_out[:, HEAD * h : HEAD * (h + 1)] = norm_back(qh[h], rqb[h], g)[:, 0:HEAD]

    ag_send(g_all, rs_sum(g_loc, g_recv, g_rs_s, g_rs_r), g_ag_s, g_ag_r)
    ag_wait(g_all, g_full, g_ag_s, g_ag_r)

    wins = jnp.zeros((DP, PAD), F32)
    for h in range(HEADS):
        rs_ = jnp.sum(s_full[h].astype(F32) * g_full[h].astype(F32), axis=1, keepdims=True)
        i_col = HEAD * h + iota((PAD, PAD), 0)
        block = (i_col * 1873) >> 16
        spot = (i_col - OWN * block == iota((PAD, PAD), 1)) & (iota((PAD, PAD), 0) < HEAD)
        spread = jnp.where(spot, jnp.broadcast_to(rs_, (PAD, PAD)), 0.0)
        i_row = HEAD * h + iota((DP, PAD), 1)
        which = jnp.where((i_row * 1873) >> 16 == iota((DP, PAD), 0), 1.0, 0.0).astype(BF)
        hi = spread.astype(BF)
        lo = (spread - hi.astype(F32)).astype(BF)
        wins = wins + dot_nn(which, hi) + dot_nn(which, lo)
    win_send[...] = wins.reshape(DP, 1, PAD)

    def win_step(o, u):
        e = (d + o) % DP
        remote(win_send.at[e], win_recv.at[o], r_s.at[o], r_r.at[o], (e, s)).start()
        return u

    lax.fori_loop(1, DP, win_step, 0)

    for h in range(HEADS):
        gqk = gain(0, h) * gain(1, h)
        g = dot_nt(vx[h], g_full[h]) * gqk
        cols = pl.ds(HEAD * h, HEAD)
        kg_out[:, cols] = norm_back(kh[h], rkb[h], g)[:, 0:HEAD]
        phi = (jnp.maximum(kh[h].astype(F32) * rkb[h], 0.0) * gqk).astype(BF)
        vg_out[:, cols] = dot_nn(phi, g_full[h])[:, 0:HEAD].astype(BF)

    def win_sum(o, acc):
        remote(win_send.at[0], win_recv.at[o], r_s.at[o], r_r.at[o], (d, s)).wait_recv()
        return acc + win_recv[o]

    total = lax.fori_loop(1, DP, win_sum, win_send[d])
    gqg_out[...] = total[:, 0:OWN] * gk_in[...]
    gkg_out[...] = total[:, 0:OWN] * gq_in[...]

    far.wait_send()

    @pl.when(c != y)
    def _():
        near.wait_send()

    og_copy.wait_send()
    gain_copy.wait_send()
    att_copy.wait_send()
    for way in range(2):
        for k in range(1, 5):
            z_copy(way, k).wait_send()
        for rel in range(1, 8):
            x_copy(way, rel).wait_send()

    def sent(o, u):
        for loc, all_, rs_, ag_ in (
            (s_loc, s_all, s_rs_s, s_ag_s),
            (g_loc, g_all, g_rs_s, g_ag_s),
        ):
            remote(loc.at[pl.ds(0, PIECE)], loc.at[pl.ds(0, PIECE)], rs_.at[o], rs_.at[o], (d, (s + o) % SEQ)).wait_send()
            remote(all_.at[s], all_.at[s], ag_.at[o], ag_.at[o], (d, (s + o) % SEQ)).wait_send()
        return u

    lax.fori_loop(1, SEQ, sent, 0)

    def win_sent(o, u):
        remote(win_send.at[0], win_recv.at[o], r_s.at[o], r_r.at[o], ((d + o) % DP, s)).wait_send()
        return u

    lax.fori_loop(1, DP, win_sent, 0)


def local(out_grad, out_weight, queries, keys, values, query_gain, key_norm_gain):
    V = pltpu.VMEM
    dma = pltpu.SemaphoreType.DMA
    any_, vm = pl.BlockSpec(memory_space=pl.ANY), pl.BlockSpec(memory_space=V)
    wide = jax.ShapeDtypeStruct((ROWS, WIDTH), BF)
    slim = jax.ShapeDtypeStruct((1, OWN), F32)
    head = (HEADS, ROWS, PAD)
    square = (HEADS, PAD, PAD)
    outs = pl.pallas_call(
        kernel,
        out_shape=(wide, wide, wide, slim, slim),
        in_specs=[any_] * 5 + [vm] * 2,
        out_specs=(vm,) * 5,
        scratch_shapes=[
            V((ROWS, WIDTH), BF), V((ROWS, WIDTH), BF), V((ROWS, WIDTH), BF),
            V((OWN, MODEL), BF), V((ROWS, MODEL), BF), V((ROWS, MODEL), BF),
            V(head, BF), V(head, BF), V(head, BF), V(head, F32), V(head, F32), V(head, BF), V(head, BF),
            V((8, 128), F32),
            V((48, 2 * HALF), BF), V((2, 48, 2 * HALF), BF),
            V((2, 8, WIN, HALF), BF), V((5 * PAD, 2 * HALF), BF),
            V((2, ROWS, 5 * PAD), BF), V((ROWS, 5 * PAD), BF), V((2, 16, 5 * PAD), F32),
            V((WIDTH, PAD), BF), V((SEQ, PIECE, PAD), BF), V((SEQ, PIECE, PAD), BF), V(square, BF),
            V((WIDTH, PAD), BF), V((SEQ, PIECE, PAD), BF), V((SEQ, PIECE, PAD), BF), V(square, BF),
            V((DP, 1, PAD), F32), V((DP, 1, PAD), F32),
            dma((5,)), dma((3,)), dma((3,)), dma((2,)), dma((2,)),
            dma((2, 4)), dma((2, 4)), dma((2, 7)), dma((2, 7)),
            *[dma((SEQ,))] * 8,
            dma((DP,)), dma((DP,)),
        ],
        compiler_params=pltpu.CompilerParams(
            collective_id=0, has_side_effects=True, vmem_limit_bytes=48 * 1024 * 1024
        ),
        cost_estimate=pl.CostEstimate(
            flops=2 * 512 * 2304 * 640, bytes_accessed=5_000_000, transcendentals=10_000
        ),
        name="attention_backward",
    )(
        out_grad[0], out_weight, queries[0], keys[0], values[0],
        query_gain.reshape(1, OWN), key_norm_gain.reshape(1, OWN),
    )
    qg, kg, vg, gq, gk = outs
    return qg[None], kg[None], vg[None], gq.reshape(OWN), gk.reshape(OWN)


def solution(mesh):
    placed = (
        P("dp", "seq", None),
        P("dp", None),
        P("dp", "seq", None),
        P("dp", "seq", None),
        P("dp", "seq", None),
        P("dp"),
        P("dp"),
    )
    return jax.shard_map(
        local,
        mesh=mesh,
        in_specs=placed,
        out_specs=(
            P("dp", "seq", None),
            P("dp", "seq", None),
            P("dp", "seq", None),
            P("dp"),
            P("dp"),
        ),
        check_vma=False,
    )
```

time: 699 us -> 102 us (0.15)
  the two profiles are of different devices: /device:TPU:8 before, /device:TPU:1 now
where the time goes in v1:
time: 102 us
  Pallas kernels  89.5 us (88%)
  local copies, waits for them, and re-layouts  11.5 us (11%)
    pallas_call x1, Pallas kernels, local(): pl.pallas_call(kernel, out_shape=(wide, wide, wide, slim, slim), in_specs...  89.5 us
    unnamed x25, local copies, waits for them, and re-layouts  11.5 us

profile of v1, /device:TPU:1, one launch (start us, length us, event | category | flops | bytes accessed | tf_op | source)
XLA Modules:
  0.0 101.8 jit_solution(2203058149471322563)
XLA Ops:
  0.6 0.0 copy-start.7
  0.6 0.0 copy-start.6
  0.7 1.4 %copy.13 = bf16[1,256,1120]{2,1,0:T(8,128)(2,1)S(1)} copy(bf16[1,256,1120]{1,2,0:T(8,128)(2,1)} %param.9) | data formatting | bytes 1146880 | tf_op args[2]
  2.1 0.0 copy-start.5
  2.1 0.0 copy-done.6
  2.1 1.1 %copy.14 = bf16[1,256,1120]{2,1,0:T(8,128)(2,1)} copy(bf16[1,256,1120]{1,2,0:T(8,128)(2,1)S(1)} %copy-done.6) | data formatting | bytes 1146880 | tf_op args[3]
  3.2 0.0 copy-done.7
  3.2 1.1 %copy.15 = bf16[1,256,1120]{2,1,0:T(8,128)(2,1)} copy(bf16[1,256,1120]{1,2,0:T(8,128)(2,1)S(1)} %copy-done.7) | data formatting | bytes 1146880 | tf_op args[4]
  4.2 0.0 copy-start.3
  4.2 0.0 copy-start.4
  4.2 0.0 copy-done.5
  4.3 0.7 copy.12
  5.0 0.0 copy-done.3
  5.0 0.0 copy-done.4
  5.0 0.0 copy-start
  5.0 1.1 %copy-done = bf16[1,256,1120]{2,1,0:T(8,128)(2,1)S(1)} copy-done((bf16[1,256,1120]{2,1,0:T(8,128)(2,1)S(1)}, bf16[1,256,1120]{2,1,0:T(8,128)(2,1)}, u32[]{:S(2)}) %copy-start) | copy-done | bytes 573464
  6.1 0.0 copy-start.1
  6.1 1.1 %copy-done.1 = bf16[1,256,1120]{2,1,0:T(8,128)(2,1)S(1)} copy-done((bf16[1,256,1120]{2,1,0:T(8,128)(2,1)S(1)}, bf16[1,256,1120]{2,1,0:T(8,128)(2,1)}, u32[]{:S(2)}) %copy-start.1) | copy-done | bytes 573464
  7.1 0.0 copy-start.2
  7.1 0.9 copy-done.2
  8.0 89.5 %attention_backward.1 = (bf16[256,1120]{1,0:T(8,128)(2,1)S(1)}, bf16[256,1120]{1,0:T(8,128)(2,1)S(1)}, bf16[256,1120]{1,0:T(8,128)(2,1)S(1)}, f32[1,35]{1,0:T(1,128)S(1)}, f32[1,35]{1,0:T(1,128)S(1)}) custom-call(bf16[256,2240]{1,0:T(8,128)(2,1)S(1)} %bitcast.11, bf16[35,2240]{1,0:T(8,128)(2,1)S(1)} %copy-done.2, bf16[256,1120]{1,0:T(8,128)(2,1)S(1)} %bitcast.15, ...), custom_call_target="tpu_custom_call" | custom-call | flops 1509949440 | bytes 5000000 | tf_op jit(solution)/shard_map/attention_backward/pallas_call | solution.py:428
  97.6 1.1 %copy.16 = bf16[1,256,1120]{1,2,0:T(8,128)(2,1)} copy(bf16[1,256,1120]{2,1,0:T(8,128)(2,1)S(1)} %bitcast.14) | data formatting | bytes 1146880
  98.6 1.1 %copy.17 = bf16[1,256,1120]{1,2,0:T(8,128)(2,1)} copy(bf16[1,256,1120]{2,1,0:T(8,128)(2,1)S(1)} %bitcast.13) | data formatting | bytes 1146880
  99.7 1.1 %copy.18 = bf16[1,256,1120]{1,2,0:T(8,128)(2,1)} copy(bf16[1,256,1120]{2,1,0:T(8,128)(2,1)S(1)} %bitcast.12) | data formatting | bytes 1146880
  100.7 0.5 copy.21
  101.2 0.5 copy.22
Async XLA Ops:
  0.6 2.6 %copy-start.7 = (bf16[1,256,1120]{1,2,0:T(8,128)(2,1)S(1)}, bf16[1,256,1120]{1,2,0:T(8,128)(2,1)}, u32[]{:S(2)}) copy-start(bf16[1,256,1120]{1,2,0:T(8,128)(2,1)} %param.11) | copy-start | bytes 1720324
  0.6 1.5 %copy-start.6 = (bf16[1,256,1120]{1,2,0:T(8,128)(2,1)S(1)}, bf16[1,256,1120]{1,2,0:T(8,128)(2,1)}, u32[]{:S(2)}) copy-start(bf16[1,256,1120]{1,2,0:T(8,128)(2,1)} %param.10) | copy-start | bytes 1720324
  2.1 2.2 %copy-start.5 = (bf16[1,256,2240]{1,2,0:T(8,128)(2,1)S(1)}, bf16[1,256,2240]{1,2,0:T(8,128)(2,1)}, u32[]{:S(2)}) copy-start(bf16[1,256,2240]{1,2,0:T(8,128)(2,1)} %param.7) | copy-start | bytes 3440644
  4.2 0.7 copy-start.3
  4.2 0.7 copy-start.4
  5.0 1.1 %copy-start = (bf16[1,256,1120]{2,1,0:T(8,128)(2,1)S(1)}, bf16[1,256,1120]{2,1,0:T(8,128)(2,1)}, u32[]{:S(2)}) copy-start(bf16[1,256,1120]{2,1,0:T(8,128)(2,1)} %copy.14) | copy-start | bytes 1720324
  6.1 1.1 %copy-start.1 = (bf16[1,256,1120]{2,1,0:T(8,128)(2,1)S(1)}, bf16[1,256,1120]{2,1,0:T(8,128)(2,1)}, u32[]{:S(2)}) copy-start(bf16[1,256,1120]{2,1,0:T(8,128)(2,1)} %copy.15) | copy-start | bytes 1720324
  7.1 0.9 copy-start.2

commit v2 on v1

v2 whole, which is shorter than its diff:
```python
import functools

import jax
import jax.numpy as jnp
from jax import lax
from jax.experimental import pallas as pl
from jax.experimental.pallas import tpu as pltpu
from jax.sharding import PartitionSpec as P

HEADS = 10
HEAD = 112
PAD = 128
ROWS = 256
WIDTH = HEADS * HEAD
MODEL = 2240
TOKENS = 4096
SEQ = 16
DP = 32
OWN = 35
HALF = 1152
CUT = 640
WIN = 80
PIECE = 80
BF = jnp.bfloat16
F32 = jnp.float32
MESH = pl.DeviceIdType.MESH


def first_tile(j):
    return (35 * j) // 8


OWNER = [max(j for j in range(SEQ) if first_tile(j) <= t) for t in range(70)]


def iota(shape, axis):
    return lax.broadcasted_iota(jnp.int32, shape, axis)


def dot_nt(a, b):
    return lax.dot_general(a, b, (((1,), (1,)), ((), ())), preferred_element_type=F32)


def dot_tn(a, b):
    return lax.dot_general(a, b, (((0,), (0,)), ((), ())), preferred_element_type=F32)


def dot_nn(a, b):
    return lax.dot_general(a, b, (((1,), (0,)), ((), ())), preferred_element_type=F32)


def kernel(
    og_in, w_in, q_in, k_in, v_in, gq_in, gk_in,
    qg_out, kg_out, vg_out, gqg_out, gkg_out,
    k_raw, q_raw, vx, w_raw, og, rk, rq, ngx,
    wpk, pair, wbuf, acc, gacc, att, att_send, gqk,
    s_loc, s_recv, s_all, s_full,
    g_loc, g_recv, g_all, g_full,
    s_own, win_send, win_recv, part_send, part_recv,
    in_sem, v_sem, misc_s, misc_r, pair_s, pair_r, z_s, z_r, x_s, x_r,
    s_rs_s, s_rs_r, s_ag_s, s_ag_r, g_rs_s, g_rs_r, g_ag_s, g_ag_r, r_s, r_r, t_s, t_r,
):
    d = lax.axis_index("dp")
    s = lax.axis_index("seq")
    y = d // 16
    z = (d // 2) % 8
    c = d % 2
    p = (s // 4) % 2
    sib = (y * 16 + z * 2 + (1 - c), s)
    up = (y * 16 + ((z + 1) % 8) * 2 + c, s)
    down = (y * 16 + ((z + 7) % 8) * 2 + c, s)
    right = (d, (s + 4) % SEQ)
    left = (d, (s + 12) % SEQ)
    far_dp = (1 - y) * 16 + z * 2
    far_seq = s - 2 * (s % 4) + 3

    def remote(src, dst, ss, rs, dev):
        return pltpu.make_async_remote_copy(
            src_ref=src, dst_ref=dst, send_sem=ss, recv_sem=rs,
            device_id=dev, device_id_type=MESH,
        )

    def head(h):
        return pl.ds(HEAD * h, HEAD)

    mine = pl.ds(0, ROWS)
    theirs = pl.ds(ROWS, ROWS)
    ins = [
        pltpu.make_async_copy(a, b, in_sem.at[i])
        for i, (a, b) in enumerate(
            ((w_in, w_raw), (k_in, k_raw), (q_in, q_raw), (og_in, og.at[pl.ds(0, MODEL), mine]))
        )
    ]
    ins_v = [
        pltpu.make_async_copy(v_in.at[head(h)], vx.at[h, pl.ds(0, HEAD)], v_sem.at[h])
        for h in range(HEADS)
    ]
    ins[0].start()
    ins[1].start()
    for cp in ins_v:
        cp.start()
    ins[2].start()
    ins[3].start()
    bar = pltpu.get_barrier_semaphore()

    def greet_seq(o, u):
        pl.semaphore_signal(bar, inc=1, device_id=(d, (s + o) % SEQ), device_id_type=MESH)
        return u

    def greet(dev):
        pl.semaphore_signal(bar, inc=1, device_id=dev, device_id_type=MESH)

    lax.fori_loop(1, SEQ, greet_seq, 0)
    greet(sib)
    greet(up)
    greet(down)

    @pl.when(c != y)
    def _():
        greet((far_dp, far_seq))
        greet((far_dp + 1, far_seq))

    ins[0].wait()
    wpk[...] = jnp.zeros_like(wpk)
    wpk[0:OWN, 0:MODEL] = w_raw[...]
    diag = iota((48, OWN), 0) == iota((48, OWN), 1)
    lane = iota((48, 64), 1)
    extra = jnp.zeros((48, 64), F32)
    for n, ref in enumerate((gq_in, gk_in)):
        col = jnp.sum(jnp.where(diag, jnp.broadcast_to(ref[...], (48, OWN)), 0.0), axis=1, keepdims=True)
        rest = col
        for m in range(3):
            part = rest.astype(BF).astype(F32)
            extra = jnp.where(lane == 3 * n + m, part, extra)
            rest = rest - part
    wpk[:, MODEL:] = extra.astype(BF)

    pl.semaphore_wait(bar, SEQ - 1 + 4)

    far = remote(wpk, pair.at[c], pair_s.at[0], pair_r.at[c], (far_dp + y, far_seq))
    near = remote(wpk, pair.at[c], pair_s.at[1], pair_r.at[c], sib)
    far.start()

    @pl.when(c != y)
    def _():
        near.start()

    @pl.when(c == y)
    def _():
        pair[c] = wpk[...]

    og_copy = remote(og_in, og.at[pl.ds(0, MODEL), theirs], misc_s.at[0], misc_r.at[0], sib)
    og_copy.start()

    ones = jnp.where(iota((16, ROWS), 0) == 0, 1.0, 0.0).astype(BF)
    og[MODEL:, :] = jnp.zeros((2 * HALF - MODEL, 2 * ROWS), BF)
    acc[...] = jnp.zeros_like(acc)
    gacc[...] = jnp.zeros_like(gacc)

    def inverse(f):
        return lax.rsqrt(jnp.sum(f * f, axis=0, keepdims=True) * (1.0 / HEAD) + 1e-06)

    ins[1].wait()
    for h in range(HEADS):
        kf = k_raw[head(h), :].astype(F32)
        r = inverse(kf)
        rk[h] = r
        phi = jnp.maximum(kf * r, 0.0).astype(BF)
        ins_v[h].wait()
        vx[h, HEAD:, :] = ones
        s_loc[head(h), :] = dot_nt(phi, vx[h]).astype(BF)

    def rs_send(loc, recv, ss, rs):
        def step(o, u):
            j = (s + o) % SEQ
            rows = pl.ds(pl.multiple_of(first_tile(j) * 16, 16), PIECE)
            remote(loc.at[rows], recv.at[o], ss.at[o], rs.at[o], (d, j)).start()
            return u

        lax.fori_loop(1, SEQ, step, 0)

    def rs_sum(loc, recv, ss, rs):
        total = loc[pl.ds(pl.multiple_of(first_tile(s) * 16, 16), PIECE), :].astype(F32)

        def step(o, total):
            remote(loc.at[pl.ds(0, PIECE)], recv.at[o], ss.at[o], rs.at[o], (d, s)).wait_recv()
            return total + recv[o].astype(F32)

        return lax.fori_loop(1, SEQ, step, total)

    def ag_send(all_, total, ss, rs):
        all_[s] = total.astype(BF)

        def step(o, u):
            remote(all_.at[s], all_.at[s], ss.at[o], rs.at[o], (d, (s + o) % SEQ)).start()
            return u

        lax.fori_loop(1, SEQ, step, 0)

    def ag_wait(all_, full, ss, rs):
        def step(o, u):
            j = (s + SEQ - o) % SEQ
            remote(all_.at[j], all_.at[j], ss.at[o], rs.at[o], (d, j)).wait_recv()
            return u

        lax.fori_loop(1, SEQ, step, 0)
        for j in range(SEQ):
            t = first_tile(j)
            n = 16 * (OWNER.count(j))
            full[16 * t : 16 * t + n, :] = all_[j, 0:n, :]

    rs_send(s_loc, s_recv, s_rs_s, s_rs_r)

    pair_wait = [remote(wpk, pair.at[i], pair_s.at[0], pair_r.at[i], sib) for i in range(2)]

    @pl.when((c != y) | (c == 1))
    def _():
        pair_wait[0].wait_recv()

    @pl.when((c != y) | (c == 0))
    def _():
        pair_wait[1].wait_recv()

    m = iota((WIN, 96), 1)
    to = (70 * z) % 16 + jnp.where(m < 48, m, m - 13)
    to = jnp.where(to >= WIN, to - WIN, to)
    good = (m < OWN) | ((m >= 48) & (m < 48 + OWN))
    place = jnp.where((iota((WIN, 96), 0) == to) & good, 1.0, 0.0).astype(BF)
    both = pair[...].reshape(96, 2 * HALF)
    window = dot_nn(place, both).astype(BF)
    wbuf[0, z] = window[:, :HALF]
    wbuf[1, z] = window[:, HALF:]

    part_a = pl.ds(0, CUT)
    part_b = pl.ds(CUT, HALF - CUT)

    def z_copy(way, k):
        b = (z - (k - 1) + 8) % 8 if way == 0 else (z + (k - 1)) % 8
        ref = wbuf.at[p, b]
        if k == 4:
            ref = wbuf.at[p, b, :, part_a if way == 0 else part_b]
        return remote(ref, ref, z_s.at[way, k - 1], z_r.at[way, k - 1], up if way == 0 else down)

    def x_copy(way, rel):
        b = (z + rel) % 8
        ref = wbuf.at[p, b, :, part_a if way == 0 else part_b]
        return remote(ref, ref, x_s.at[way, rel - 1], x_r.at[way, rel - 1], right if way == 0 else left)

    def x_wait(way, rel):
        b = (z + rel) % 8
        ref = wbuf.at[1 - p, b, :, part_a if way == 0 else part_b]
        remote(ref, ref, x_s.at[way, rel - 1], x_r.at[way, rel - 1], right).wait_recv()

    def z_step(k):
        z_copy(0, k).wait_recv()
        if k < 4:
            z_copy(0, k + 1).start()
            x_copy(0, 8 - k).start()
            x_copy(1, 8 - k).start()
        else:
            x_copy(0, 4).start()
        z_copy(1, k).wait_recv()
        if k < 4:
            z_copy(1, k + 1).start()
            x_copy(0, k).start()
            x_copy(1, k).start()
        else:
            x_copy(1, 4).start()

    z_copy(0, 1).start()
    z_copy(1, 1).start()

    row = iota((16, 1), 0)
    er = iota((128, 256), 0)
    el = iota((128, 256), 1)
    pick = ((er >= 64) & (er < 67) & (el < 128)) | ((er >= 67) & (er < 70) & (el >= 128))

    def add_rows(ref, b, res):
        start = pl.multiple_of(((70 * b) // 16) * 16, 16)
        phase = (70 * b) % 16
        over = phase + 70 - WIN
        ref[pl.ds(start, 16), :] += jnp.where(row >= phase, res[0:16], 0.0)
        ref[pl.ds(start + 16, WIN - 16), :] += res[16:]
        ref[pl.ds(start + WIN, 16), :] += jnp.where(row < over, res[0:16], 0.0)

    def product(e, b):
        rows = pl.ds(pl.multiple_of(e * HALF, 128), HALF)
        add_rows(acc, b, dot_nn(wbuf[e, b], og[rows, :]))
        spread = jnp.where(pick & (e == 1), 1.0, 0.0).astype(BF)
        add_rows(gacc, b, dot_nn(wbuf[e, b, :, HALF - 128 :], spread))

    ins[2].wait()
    for h in range(HEADS):
        rq[h] = inverse(q_raw[head(h), :].astype(F32))

    z_step(1)
    s_own[...] = rs_sum(s_loc, s_recv, s_rs_s, s_rs_r)
    ag_send(s_all, s_own[...], s_ag_s, s_ag_r)
    ins[3].wait()
    og_copy.wait_recv()
    product(p, z)
    product(1 - p, z)
    z_step(2)
    product(p, (z + 1) % 8)
    product(p, (z + 7) % 8)
    z_step(3)
    product(p, (z + 2) % 8)
    product(p, (z + 6) % 8)
    ag_wait(s_all, s_full, s_ag_s, s_ag_r)
    z_step(4)
    product(p, (z + 3) % 8)
    product(p, (z + 5) % 8)
    for rel in (1, 7, 2, 6, 3, 5):
        x_wait(0, rel)
        x_wait(1, rel)
        product(1 - p, (z + rel) % 8)
    product(p, (z + 4) % 8)
    x_wait(0, 4)
    x_wait(1, 4)
    product(1 - p, (z + 4) % 8)

    half_heads = 5 * HEAD
    att_send[...] = acc[0:half_heads, ROWS:].astype(BF)
    att_copy = remote(att_send, att.at[c], misc_s.at[2], misc_r.at[2], sib)
    att_copy.start()
    gqk[c] = gacc[0:half_heads, 0:128] * gacc[0:half_heads, 128:]
    gain_copy = remote(gqk.at[c], gqk.at[c], misc_s.at[1], misc_r.at[1], sib)
    gain_copy.start()
    att[c] = acc[0:half_heads, 0:ROWS].astype(BF)
    remote(gqk.at[1 - c], gqk.at[1 - c], misc_s.at[1], misc_r.at[1], sib).wait_recv()
    remote(att_send, att.at[1 - c], misc_s.at[2], misc_r.at[2], sib).wait_recv()

    def gain(h):
        g = gqk[h // 5, HEAD * (h % 5) : HEAD * (h % 5 + 1), :]
        return jnp.concatenate([g, g], axis=1)

    first = iota((16, ROWS), 0) == 0
    for h in range(HEADS):
        phi = jnp.maximum(q_raw[head(h), :].astype(F32) * rq[h], 0.0)
        num = dot_tn(s_full[head(h), :], (phi * gain(h)).astype(BF))
        inv = 1.0 / (num[HEAD : HEAD + 1] + float(TOKENS))
        ng = att[h // 5, HEAD * (h % 5) : HEAD * (h % 5 + 1), :].astype(F32) * inv
        dg = -jnp.sum(ng * num[0:HEAD], axis=0, keepdims=True) * inv
        ngx[h, 0:HEAD, :] = ng.astype(BF)
        ngx[h, HEAD:, :] = jnp.where(first, dg, 0.0).astype(BF)
        g_loc[head(h), :] = dot_nt(phi.astype(BF), ngx[h]).astype(BF)

    rs_send(g_loc, g_recv, g_rs_s, g_rs_r)

    def norm_back(raw, r, grad):
        f = raw.astype(F32)
        a = jnp.where(f > 0, grad, 0.0)
        hat = f * r
        mean = jnp.sum(a * hat, axis=0, keepdims=True) * (1.0 / HEAD)
        return (r * (a - hat * mean)).astype(BF)

    g_sum = rs_sum(g_loc, g_recv, g_rs_s, g_rs_r)
    ag_send(g_all, g_sum, g_ag_s, g_ag_r)
    sums = jnp.sum(g_sum * s_own[...], axis=1, keepdims=True)
    lanes = jnp.where(iota((PIECE, PAD), 0) == iota((PIECE, PAD), 1), jnp.broadcast_to(sums, (PIECE, PAD)), 0.0)
    win_send[...] = jnp.sum(lanes, axis=0, keepdims=True)

    def win_copy(o):
        return remote(win_send, win_recv.at[o], r_s.at[o], r_r.at[o], ((d + o) % DP, s))

    def win_step(o, u):
        win_copy(o).start()
        return u

    lax.fori_loop(1, DP, win_step, 0)

    for h in range(HEADS):
        g = dot_nn(s_full[head(h), :], ngx[h]) * gain(h)
        qg_out[head(h), :] = norm_back(q_raw[head(h), :], rq[h], g)

    def win_sum(o, total):
        win_copy(o).wait_recv()
        return total + win_recv[o]

    total = lax.fori_loop(1, DP, win_sum, win_send[...])
    own_first = first_tile(s)
    own_rows = 16 * (jnp.where(s == SEQ - 1, 70, first_tile(s + 1)) - own_first)
    at = iota((PAD, PAD), 1)
    spot = (at + 16 * own_first - OWN * d == iota((PAD, PAD), 0)) & (at < own_rows)
    spot = spot & (iota((PAD, PAD), 0) < OWN)
    col = jnp.sum(jnp.where(spot, jnp.broadcast_to(total, (PAD, PAD)), 0.0), axis=1, keepdims=True)
    across = jnp.where(iota((PAD, PAD), 0) == at, jnp.broadcast_to(col, (PAD, PAD)), 0.0)
    part_send[...] = jnp.sum(across, axis=0, keepdims=True)

    def part_copy(o):
        return remote(part_send, part_recv.at[o], t_s.at[o], t_r.at[o], (d, (s + o) % SEQ))

    def part_step(o, u):
        part_copy(o).start()
        return u

    lax.fori_loop(1, SEQ, part_step, 0)
    ag_wait(g_all, g_full, g_ag_s, g_ag_r)

    for h in range(HEADS):
        gg = gain(h)
        kf = k_raw[head(h), :].astype(F32)
        g = dot_nn(g_full[head(h), :], vx[h]) * gg
        kg_out[head(h), :] = norm_back(k_raw[head(h), :], rk[h], g)
        phi = (jnp.maximum(kf * rk[h], 0.0) * gg).astype(BF)
        vg_out[head(h), :] = dot_tn(g_full[head(h), :], phi)[0:HEAD].astype(BF)

    def part_sum(o, total):
        part_copy(o).wait_recv()
        return total + part_recv[o]

    total = lax.fori_loop(1, SEQ, part_sum, part_send[...])
    gqg_out[...] = total[:, 0:OWN] * gk_in[...]
    gkg_out[...] = total[:, 0:OWN] * gq_in[...]

    far.wait_send()

    @pl.when(c != y)
    def _():
        near.wait_send()

    og_copy.wait_send()
    gain_copy.wait_send()
    att_copy.wait_send()
    for way in range(2):
        for k in range(1, 5):
            z_copy(way, k).wait_send()
        for rel in range(1, 8):
            x_copy(way, rel).wait_send()

    def sent(o, u):
        for loc, all_, rs_, ag_ in (
            (s_loc, s_all, s_rs_s, s_ag_s),
            (g_loc, g_all, g_rs_s, g_ag_s),
        ):
            part = loc.at[pl.ds(0, PIECE)]
            remote(part, part, rs_.at[o], rs_.at[o], (d, (s + o) % SEQ)).wait_send()
            remote(all_.at[s], all_.at[s], ag_.at[o], ag_.at[o], (d, (s + o) % SEQ)).wait_send()
        return u

    lax.fori_loop(1, SEQ, sent, 0)

    def win_sent(o, u):
        win_copy(o).wait_send()
        return u

    lax.fori_loop(1, DP, win_sent, 0)

    def part_sent(o, u):
        part_copy(o).wait_send()
        return u

    lax.fori_loop(1, SEQ, part_sent, 0)


def local(out_grad, out_weight, queries, keys, values, query_gain, key_norm_gain):
    V = pltpu.VMEM
    dma = pltpu.SemaphoreType.DMA
    any_, vm = pl.BlockSpec(memory_space=pl.ANY), pl.BlockSpec(memory_space=V)
    wide = jax.ShapeDtypeStruct((WIDTH, ROWS), BF)
    slim = jax.ShapeDtypeStruct((1, OWN), F32)
    summed = [
        V((WIDTH, PAD), BF), V((SEQ, PIECE, PAD), BF), V((SEQ, PIECE, PAD), BF), V((WIDTH, PAD), BF),
    ]
    outs = pl.pallas_call(
        kernel,
        out_shape=(wide, wide, wide, slim, slim),
        in_specs=[any_] * 5 + [vm] * 2,
        out_specs=(vm,) * 5,
        scratch_shapes=[
            V((WIDTH, ROWS), BF), V((WIDTH, ROWS), BF), V((HEADS, PAD, ROWS), BF),
            V((OWN, MODEL), BF), V((2 * HALF, 2 * ROWS), BF),
            V((HEADS, 1, ROWS), F32), V((HEADS, 1, ROWS), F32), V((HEADS, PAD, ROWS), BF),
            V((48, 2 * HALF), BF), V((2, 48, 2 * HALF), BF), V((2, 8, WIN, HALF), BF),
            V((5 * HEAD + 32, 2 * ROWS), F32), V((5 * HEAD + 32, 256), F32),
            V((2, 5 * HEAD, ROWS), BF), V((5 * HEAD, ROWS), BF), V((2, 5 * HEAD, PAD), F32),
            *summed, *summed,
            V((PIECE, PAD), F32), V((1, PAD), F32), V((DP, 1, PAD), F32), V((1, PAD), F32), V((SEQ, 1, PAD), F32),
            dma((4,)), dma((HEADS,)), dma((3,)), dma((3,)), dma((2,)), dma((2,)),
            dma((2, 4)), dma((2, 4)), dma((2, 7)), dma((2, 7)),
            *[dma((SEQ,))] * 8,
            dma((DP,)), dma((DP,)), dma((SEQ,)), dma((SEQ,)),
        ],
        compiler_params=pltpu.CompilerParams(
            collective_id=0, has_side_effects=True, vmem_limit_bytes=63 * 1024 * 1024
        ),
        cost_estimate=pl.CostEstimate(
            flops=2 * 512 * 2304 * 640, bytes_accessed=5_000_000, transcendentals=10_000
        ),
        name="attention_backward",
    )(
        out_grad[0].T, out_weight, queries[0].T, keys[0].T, values[0].T,
        query_gain.reshape(1, OWN), key_norm_gain.reshape(1, OWN),
    )
    qg, kg, vg, gq, gk = outs
    return qg.T[None], kg.T[None], vg.T[None], gq.reshape(OWN), gk.reshape(OWN)


def solution(mesh):
    placed = (
        P("dp", "seq", None),
        P("dp", None),
        P("dp", "seq", None),
        P("dp", "seq", None),
        P("dp", "seq", None),
        P("dp"),
        P("dp"),
    )
    return jax.shard_map(
        local,
        mesh=mesh,
        in_specs=placed,
        out_specs=(
            P("dp", "seq", None),
            P("dp", "seq", None),
            P("dp", "seq", None),
            P("dp"),
            P("dp"),
        ),
        check_vma=False,
    )
```

time: 102 us -> 86.4 us (0.85)
  Pallas kernels: 89.5 us -> 80.9 us
  local copies, waits for them, and re-layouts: 11.5 us -> 4.65 us
    pallas_call x1, Pallas kernels: 89.5 us -> 80.9 us  [local(): pl.pallas_call(kernel, out_shape=(wide, wide, wide, slim, slim), in_specs...]
    unnamed x25 -> x13, local copies, waits for them, and re-layouts: 11.5 us -> 4.65 us
where the time goes in v2:
time: 86.4 us; the launch traced here: 86.3 us
  Pallas kernels  80.9 us (94%)
  local copies, waits for them, and re-layouts  4.65 us (5%)
    pallas_call x1, Pallas kernels, local(): pl.pallas_call(kernel, out_shape=(wide, wide, wide, slim, slim), in_specs...  80.9 us
    unnamed x13, local copies, waits for them, and re-layouts  4.65 us

profile of v2, /device:TPU:1, one launch (start us, length us, event | category | flops | bytes accessed | tf_op | source)
XLA Modules:
  0.0 86.3 jit_solution(16498263632536244081)
XLA Ops:
  0.6 80.9 %attention_backward.1 = (bf16[1120,256]{1,0:T(8,128)(2,1)}, bf16[1120,256]{1,0:T(8,128)(2,1)}, bf16[1120,256]{1,0:T(8,128)(2,1)}, f32[1,35]{1,0:T(1,128)}, f32[1,35]{1,0:T(1,128)}) custom-call(bf16[2240,256]{1,0:T(8,128)(2,1)} %bitcast.28, bf16[35,2240]{1,0:T(8,128)(2,1)} %w_in.1, bf16[1120,256]{1,0:T(8,128)(2,1)} %bitcast.29, bf16[1120,256]{1,0:T(8,128)(2,1)} %bitcast.30, ...), custom_call_target="tpu_custom_call" | custom-call | flops 1509949440 | bytes 5000000 | tf_op jit(solution)/shard_map/attention_backward/pallas_call | solution.py:465
  81.6 0.0 copy-start.1
  81.6 0.0 copy-start
  81.6 2.0 %copy.17 = bf16[1,256,1120]{1,2,0:T(8,128)(2,1)} copy(bf16[1,256,1120]{1,2,0:T(8,128)(2,1)} %bitcast.27) | data formatting | bytes 1146880
  83.6 0.0 copy-done.1
  83.6 0.0 copy-start.3
  83.6 0.0 copy-start.2
  83.6 0.8 copy.18
  84.4 0.0 copy-done
  84.4 0.8 copy.19
  85.2 0.0 copy-done.3
  85.2 0.5 copy.20
  85.8 0.0 copy-done.2
  85.8 0.5 copy.21
Async XLA Ops:
  81.6 2.0 %copy-start.1 = (bf16[1120,256]{1,0:T(8,128)(2,1)S(1)}, bf16[1120,256]{1,0:T(8,128)(2,1)}, u32[]{:S(2)}) copy-start(bf16[1120,256]{1,0:T(8,128)(2,1)} %get-tuple-element.11) | copy-start | bytes 1720324
  81.6 2.8 %copy-start = (bf16[1120,256]{1,0:T(8,128)(2,1)S(1)}, bf16[1120,256]{1,0:T(8,128)(2,1)}, u32[]{:S(2)}) copy-start(bf16[1120,256]{1,0:T(8,128)(2,1)} %get-tuple-element.12) | copy-start | bytes 1720324
  83.6 1.6 %copy-start.3 = (f32[1,35]{1,0:T(1,128)S(1)}, f32[1,35]{1,0:T(1,128)}, u32[]{:S(2)}) copy-start(f32[1,35]{1,0:T(1,128)} %get-tuple-element.13) | copy-start | bytes 424
  83.6 2.1 %copy-start.2 = (f32[1,35]{1,0:T(1,128)S(1)}, f32[1,35]{1,0:T(1,128)}, u32[]{:S(2)}) copy-start(f32[1,35]{1,0:T(1,128)} %get-tuple-element.14) | copy-start | bytes 424

commit v3 on v2

--- a/solution.py
+++ b/solution.py
@@ -18,19 +18,23 @@
 DP = 32
 OWN = 35
 HALF = 1152
-CUT = 640
+CUT = 384
+PARTS = HALF // CUT
 WIN = 80
 PIECE = 80
+GROUPS = ((0, 42, 3, 0), (672, 28, 2, 48))
 BF = jnp.bfloat16
 F32 = jnp.float32
 MESH = pl.DeviceIdType.MESH
 
 
-def first_tile(j):
-    return (35 * j) // 8
-
-
-OWNER = [max(j for j in range(SEQ) if first_tile(j) <= t) for t in range(70)]
+def first_tile(group, j):
+    return (group[1] * j) // SEQ
+
+
+OWNER = [
+    [max(j for j in range(SEQ) if first_tile(g, j) <= t) for t in range(g[1])] for g in GROUPS
+]
 
 
 def iota(shape, axis):
@@ -56,7 +60,7 @@
     wpk, pair, wbuf, acc, gacc, att, att_send, gqk,
     s_loc, s_recv, s_all, s_full,
     g_loc, g_recv, g_all, g_full,
-    s_own, win_send, win_recv, part_send, part_recv,
+    win_send, win_recv, part_send, part_recv,
     in_sem, v_sem, misc_s, misc_r, pair_s, pair_r, z_s, z_r, x_s, x_r,
     s_rs_s, s_rs_r, s_ag_s, s_ag_r, g_rs_s, g_rs_r, g_ag_s, g_ag_r, r_s, r_r, t_s, t_r,
 ):
@@ -135,23 +139,6 @@
             rest = rest - part
     wpk[:, MODEL:] = extra.astype(BF)
 
-    pl.semaphore_wait(bar, SEQ - 1 + 4)
-
-    far = remote(wpk, pair.at[c], pair_s.at[0], pair_r.at[c], (far_dp + y, far_seq))
-    near = remote(wpk, pair.at[c], pair_s.at[1], pair_r.at[c], sib)
-    far.start()
-
-    @pl.when(c != y)
-    def _():
-        near.start()
-
-    @pl.when(c == y)
-    def _():
-        pair[c] = wpk[...]
-
-    og_copy = remote(og_in, og.at[pl.ds(0, MODEL), theirs], misc_s.at[0], misc_r.at[0], sib)
-    og_copy.start()
-
     ones = jnp.where(iota((16, ROWS), 0) == 0, 1.0, 0.0).astype(BF)
     og[MODEL:, :] = jnp.zeros((2 * HALF - MODEL, 2 * ROWS), BF)
     acc[...] = jnp.zeros_like(acc)
@@ -160,56 +147,101 @@
     def inverse(f):
         return lax.rsqrt(jnp.sum(f * f, axis=0, keepdims=True) * (1.0 / HEAD) + 1e-06)
 
-    ins[1].wait()
-    for h in range(HEADS):
-        kf = k_raw[head(h), :].astype(F32)
-        r = inverse(kf)
-        rk[h] = r
-        phi = jnp.maximum(kf * r, 0.0).astype(BF)
-        ins_v[h].wait()
-        vx[h, HEAD:, :] = ones
-        s_loc[head(h), :] = dot_nt(phi, vx[h]).astype(BF)
-
-    def rs_send(loc, recv, ss, rs):
+    def piece_rows(g):
+        return pl.ds(g[3], 16 * g[2])
+
+    def rs_copy(i, sums, o):
+        g = GROUPS[i]
+        j = (s + o) % SEQ
+        rows = pl.ds(pl.multiple_of(g[0] + first_tile(g, j) * 16, 16), 16 * g[2])
+        return remote(sums[0].at[rows], sums[1].at[o, piece_rows(g)], sums[4].at[i, o], sums[5].at[i, o], (d, j))
+
+    def ag_copy(i, sums, o, j):
+        piece = sums[2].at[j, piece_rows(GROUPS[i])]
+        return remote(piece, piece, sums[6].at[i, o], sums[7].at[i, o], (d, (s + o) % SEQ))
+
+    def rs_send(i, sums):
         def step(o, u):
-            j = (s + o) % SEQ
-            rows = pl.ds(pl.multiple_of(first_tile(j) * 16, 16), PIECE)
-            remote(loc.at[rows], recv.at[o], ss.at[o], rs.at[o], (d, j)).start()
+            rs_copy(i, sums, o).start()
             return u
 
         lax.fori_loop(1, SEQ, step, 0)
 
-    def rs_sum(loc, recv, ss, rs):
-        total = loc[pl.ds(pl.multiple_of(first_tile(s) * 16, 16), PIECE), :].astype(F32)
+    def rs_sum(i, sums):
+        g = GROUPS[i]
+        rows = pl.ds(pl.multiple_of(g[0] + first_tile(g, s) * 16, 16), 16 * g[2])
 
         def step(o, total):
-            remote(loc.at[pl.ds(0, PIECE)], recv.at[o], ss.at[o], rs.at[o], (d, s)).wait_recv()
-            return total + recv[o].astype(F32)
-
-        return lax.fori_loop(1, SEQ, step, total)
-
-    def ag_send(all_, total, ss, rs):
-        all_[s] = total.astype(BF)
+            rs_copy(i, sums, o).wait_recv()
+            return total + sums[1][o, g[3] : g[3] + 16 * g[2], :].astype(F32)
+
+        return lax.fori_loop(1, SEQ, step, sums[0][rows, :].astype(F32))
+
+    def ag_send(i, sums, total):
+        g = GROUPS[i]
+        sums[2][s, g[3] : g[3] + 16 * g[2], :] = total.astype(BF)
 
         def step(o, u):
-            remote(all_.at[s], all_.at[s], ss.at[o], rs.at[o], (d, (s + o) % SEQ)).start()
+            ag_copy(i, sums, o, s).start()
             return u
 
         lax.fori_loop(1, SEQ, step, 0)
 
-    def ag_wait(all_, full, ss, rs):
+    def ag_wait(i, sums):
+        g = GROUPS[i]
+
         def step(o, u):
-            j = (s + SEQ - o) % SEQ
-            remote(all_.at[j], all_.at[j], ss.at[o], rs.at[o], (d, j)).wait_recv()
+            ag_copy(i, sums, o, (s + SEQ - o) % SEQ).wait_recv()
             return u
 
         lax.fori_loop(1, SEQ, step, 0)
         for j in range(SEQ):
-            t = first_tile(j)
-            n = 16 * (OWNER.count(j))
-            full[16 * t : 16 * t + n, :] = all_[j, 0:n, :]
-
-    rs_send(s_loc, s_recv, s_rs_s, s_rs_r)
+            row = g[0] + 16 * first_tile(g, j)
+            n = 16 * OWNER[i].count(j)
+            sums[3][row : row + n, :] = sums[2][j, g[3] : g[3] + n, :]
+
+    s_sums = (s_loc, s_recv, s_all, s_full, s_rs_s, s_rs_r, s_ag_s, s_ag_r)
+    g_sums = (g_loc, g_recv, g_all, g_full, g_rs_s, g_rs_r, g_ag_s, g_ag_r)
+
+    def summary():
+        ins[1].wait()
+        for h in range(HEADS):
+            ins_v[h].wait()
+        vx[:, HEAD:, :] = jnp.broadcast_to(ones, (HEADS, PAD - HEAD, ROWS))
+        for h in range(HEADS):
+            kf = k_raw[head(h), :].astype(F32)
+            r = inverse(kf)
+            rk[h] = r
+            phi = jnp.maximum(kf * r, 0.0).astype(BF)
+            s_loc[head(h), :] = dot_nt(phi, vx[h]).astype(BF)
+
+    early = z < 4
+
+    @pl.when(early)
+    def _():
+        summary()
+
+    pl.semaphore_wait(bar, SEQ - 1 + 4)
+
+    far = remote(wpk, pair.at[c], pair_s.at[0], pair_r.at[c], (far_dp + y, far_seq))
+    near = remote(wpk, pair.at[c], pair_s.at[1], pair_r.at[c], sib)
+    far.start()
+
+    @pl.when(c != y)
+    def _():
+        near.start()
+
+    @pl.when(c == y)
+    def _():
+        pair[c] = wpk[...]
+
+    og_copy = remote(og_in, og.at[pl.ds(0, MODEL), theirs], misc_s.at[0], misc_r.at[0], sib)
+    og_copy.start()
+
+    @pl.when(early)
+    def _():
+        rs_send(0, s_sums)
+        rs_send(1, s_sums)
 
     pair_wait = [remote(wpk, pair.at[i], pair_s.at[0], pair_r.at[i], sib) for i in range(2)]
 
@@ -231,44 +263,44 @@
     wbuf[0, z] = window[:, :HALF]
     wbuf[1, z] = window[:, HALF:]
 
-    part_a = pl.ds(0, CUT)
-    part_b = pl.ds(CUT, HALF - CUT)
-
-    def z_copy(way, k):
+    def part(e, b, q):
+        return wbuf.at[e, b, :, pl.ds(CUT * q, CUT)]
+
+    def z_copy(way, k, q):
         b = (z - (k - 1) + 8) % 8 if way == 0 else (z + (k - 1)) % 8
-        ref = wbuf.at[p, b]
-        if k == 4:
-            ref = wbuf.at[p, b, :, part_a if way == 0 else part_b]
-        return remote(ref, ref, z_s.at[way, k - 1], z_r.at[way, k - 1], up if way == 0 else down)
-
-    def x_copy(way, rel):
-        b = (z + rel) % 8
-        ref = wbuf.at[p, b, :, part_a if way == 0 else part_b]
-        return remote(ref, ref, x_s.at[way, rel - 1], x_r.at[way, rel - 1], right if way == 0 else left)
-
-    def x_wait(way, rel):
-        b = (z + rel) % 8
-        ref = wbuf.at[1 - p, b, :, part_a if way == 0 else part_b]
-        remote(ref, ref, x_s.at[way, rel - 1], x_r.at[way, rel - 1], right).wait_recv()
+        ref = part(p, b, q)
+        return remote(ref, ref, z_s.at[way, k - 1, q], z_r.at[way, k - 1, q], up if way == 0 else down)
+
+    def x_copy(rel, q):
+        ref = part(p, (z + rel) % 8, q)
+        return remote(ref, ref, x_s.at[rel - 1, q], x_r.at[rel - 1, q], right if (q + rel) % 2 == 0 else left)
+
+    def x_wait(rel):
+        for q in range(PARTS):
+            ref = part(1 - p, (z + rel) % 8, q)
+            remote(ref, ref, x_s.at[rel - 1, q], x_r.at[rel - 1, q], right).wait_recv()
+
+    def goes(way, k, q):
+        return k < 4 or q % 2 == way
 
     def z_step(k):
-        z_copy(0, k).wait_recv()
-        if k < 4:
-            z_copy(0, k + 1).start()
-            x_copy(0, 8 - k).start()
-            x_copy(1, 8 - k).start()
-        else:
-            x_copy(0, 4).start()
-        z_copy(1, k).wait_recv()
-        if k < 4:
-            z_copy(1, k + 1).start()
-            x_copy(0, k).start()
-            x_copy(1, k).start()
-        else:
-            x_copy(1, 4).start()
-
-    z_copy(0, 1).start()
-    z_copy(1, 1).start()
+        for q in range(PARTS):
+            for way in range(2):
+                if goes(way, k, q):
+                    z_copy(way, k, q).wait_recv()
+                    if k < 4 and goes(way, k + 1, q):
+                        z_copy(way, k + 1, q).start()
+                    x_copy(8 - k if way == 0 else k, q).start()
+
+    for q in range(PARTS):
+        z_copy(0, 1, q).start()
+        z_copy(1, 1, q).start()
+
+    @pl.when(z >= 4)
+    def _():
+        summary()
+        rs_send(0, s_sums)
+        rs_send(1, s_sums)
 
     row = iota((16, 1), 0)
     er = iota((128, 256), 0)
@@ -293,31 +325,38 @@
     for h in range(HEADS):
         rq[h] = inverse(q_raw[head(h), :].astype(F32))
 
+    def spread_summary():
+        for i in range(2):
+            ag_send(i, s_sums, rs_sum(i, s_sums))
+
+    @pl.when(early)
+    def _():
+        spread_summary()
+
     z_step(1)
-    s_own[...] = rs_sum(s_loc, s_recv, s_rs_s, s_rs_r)
-    ag_send(s_all, s_own[...], s_ag_s, s_ag_r)
+    z_step(2)
+
+    @pl.when(z >= 4)
+    def _():
+        spread_summary()
+
     ins[3].wait()
     og_copy.wait_recv()
     product(p, z)
     product(1 - p, z)
-    z_step(2)
-    product(p, (z + 1) % 8)
-    product(p, (z + 7) % 8)
     z_step(3)
-    product(p, (z + 2) % 8)
-    product(p, (z + 6) % 8)
-    ag_wait(s_all, s_full, s_ag_s, s_ag_r)
+    for rel in (1, 7, 2, 6):
+        product(p, (z + rel) % 8)
     z_step(4)
-    product(p, (z + 3) % 8)
-    product(p, (z + 5) % 8)
-    for rel in (1, 7, 2, 6, 3, 5):
-        x_wait(0, rel)
-        x_wait(1, rel)
+    ag_wait(0, s_sums)
+    ag_wait(1, s_sums)
+    for rel in (1, 7, 2, 6):
+        x_wait(rel)
         product(1 - p, (z + rel) % 8)
-    product(p, (z + 4) % 8)
-    x_wait(0, 4)
-    x_wait(1, 4)
-    product(1 - p, (z + 4) % 8)
+    for rel in (3, 5, 4):
+        product(p, (z + rel) % 8)
+        x_wait(rel)
+        product(1 - p, (z + rel) % 8)
 
     half_heads = 5 * HEAD
     att_send[...] = acc[0:half_heads, ROWS:].astype(BF)
@@ -335,7 +374,7 @@
         return jnp.concatenate([g, g], axis=1)
 
     first = iota((16, ROWS), 0) == 0
-    for h in range(HEADS):
+    def grads_of(h):
         phi = jnp.maximum(q_raw[head(h), :].astype(F32) * rq[h], 0.0)
         num = dot_tn(s_full[head(h), :], (phi * gain(h)).astype(BF))
         inv = 1.0 / (num[HEAD : HEAD + 1] + float(TOKENS))
@@ -343,9 +382,36 @@
         dg = -jnp.sum(ng * num[0:HEAD], axis=0, keepdims=True) * inv
         ngx[h, 0:HEAD, :] = ng.astype(BF)
         ngx[h, HEAD:, :] = jnp.where(first, dg, 0.0).astype(BF)
-        g_loc[head(h), :] = dot_nt(phi.astype(BF), ngx[h]).astype(BF)
-
-    rs_send(g_loc, g_recv, g_rs_s, g_rs_r)
+        local = dot_nt(phi.astype(BF), ngx[h])
+        g_loc[head(h), :] = local.astype(BF)
+        sums = jnp.sum(local * s_full[head(h), :].astype(F32), axis=1, keepdims=True)
+        i_col = HEAD * h + iota((HEAD, PAD), 0)
+        spot = i_col - OWN * ((i_col * 1873) >> 16) == iota((HEAD, PAD), 1)
+        spread = jnp.where(spot, jnp.broadcast_to(sums, (HEAD, PAD)), 0.0)
+        i_row = HEAD * h + iota((DP, HEAD), 1)
+        which = jnp.where((i_row * 1873) >> 16 == iota((DP, HEAD), 0), 1.0, 0.0).astype(BF)
+        hi = spread.astype(BF)
+        lo = (spread - hi.astype(F32)).astype(BF)
+        return dot_nn(which, hi) + dot_nn(which, lo)
+
+    wins = jnp.zeros((DP, PAD), F32)
+    for h in range(0, 6):
+        wins = wins + grads_of(h)
+    rs_send(0, g_sums)
+    for h in range(6, HEADS):
+        wins = wins + grads_of(h)
+    rs_send(1, g_sums)
+    win_send[...] = wins.reshape(DP, 1, PAD)
+
+    def win_copy(o):
+        e = (d + o) % DP
+        return remote(win_send.at[e], win_recv.at[o], r_s.at[o], r_r.at[o], (e, s))
+
+    def win_step(o, u):
+        win_copy(o).start()
+        return u
+
+    lax.fori_loop(1, DP, win_step, 0)
 
     def norm_back(raw, r, grad):
         f = raw.astype(F32)
@@ -354,38 +420,21 @@
         mean = jnp.sum(a * hat, axis=0, keepdims=True) * (1.0 / HEAD)
         return (r * (a - hat * mean)).astype(BF)
 
-    g_sum = rs_sum(g_loc, g_recv, g_rs_s, g_rs_r)
-    ag_send(g_all, g_sum, g_ag_s, g_ag_r)
-    sums = jnp.sum(g_sum * s_own[...], axis=1, keepdims=True)
-    lanes = jnp.where(iota((PIECE, PAD), 0) == iota((PIECE, PAD), 1), jnp.broadcast_to(sums, (PIECE, PAD)), 0.0)
-    win_send[...] = jnp.sum(lanes, axis=0, keepdims=True)
-
-    def win_copy(o):
-        return remote(win_send, win_recv.at[o], r_s.at[o], r_r.at[o], ((d + o) % DP, s))
-
-    def win_step(o, u):
-        win_copy(o).start()
-        return u
-
-    lax.fori_loop(1, DP, win_step, 0)
-
-    for h in range(HEADS):
+    def query_grad(h):
         g = dot_nn(s_full[head(h), :], ngx[h]) * gain(h)
         qg_out[head(h), :] = norm_back(q_raw[head(h), :], rq[h], g)
+
+    for h in range(HEADS):
+        query_grad(h)
+
+    for i in range(2):
+        ag_send(i, g_sums, rs_sum(i, g_sums))
 
     def win_sum(o, total):
         win_copy(o).wait_recv()
         return total + win_recv[o]
 
-    total = lax.fori_loop(1, DP, win_sum, win_send[...])
-    own_first = first_tile(s)
-    own_rows = 16 * (jnp.where(s == SEQ - 1, 70, first_tile(s + 1)) - own_first)
-    at = iota((PAD, PAD), 1)
-    spot = (at + 16 * own_first - OWN * d == iota((PAD, PAD), 0)) & (at < own_rows)
-    spot = spot & (iota((PAD, PAD), 0) < OWN)
-    col = jnp.sum(jnp.where(spot, jnp.broadcast_to(total, (PAD, PAD)), 0.0), axis=1, keepdims=True)
-    across = jnp.where(iota((PAD, PAD), 0) == at, jnp.broadcast_to(col, (PAD, PAD)), 0.0)
-    part_send[...] = jnp.sum(across, axis=0, keepdims=True)
+    part_send[...] = lax.fori_loop(1, DP, win_sum, win_send[d])
 
     def part_copy(o):
         return remote(part_send, part_recv.at[o], t_s.at[o], t_r.at[o], (d, (s + o) % SEQ))
@@ -395,9 +444,7 @@
         return u
 
     lax.fori_loop(1, SEQ, part_step, 0)
-    ag_wait(g_all, g_full, g_ag_s, g_ag_r)
-
-    for h in range(HEADS):
+    def key_grad(h):
         gg = gain(h)
         kf = k_raw[head(h), :].astype(F32)
         g = dot_nn(g_full[head(h), :], vx[h]) * gg
@@ -405,6 +452,13 @@
         phi = (jnp.maximum(kf * rk[h], 0.0) * gg).astype(BF)
         vg_out[head(h), :] = dot_tn(g_full[head(h), :], phi)[0:HEAD].astype(BF)
 
+    ag_wait(0, g_sums)
+    for h in range(0, 6):
+        key_grad(h)
+    ag_wait(1, g_sums)
+    for h in range(6, HEADS):
+        key_grad(h)
+
     def part_sum(o, total):
         part_copy(o).wait_recv()
         return total + part_recv[o]
@@ -422,20 +476,19 @@
     og_copy.wait_send()
     gain_copy.wait_send()
     att_copy.wait_send()
-    for way in range(2):
-        for k in range(1, 5):
-            z_copy(way, k).wait_send()
+    for q in range(PARTS):
+        for way in range(2):
+            for k in range(1, 5):
+                if goes(way, k, q):
+                    z_copy(way, k, q).wait_send()
         for rel in range(1, 8):
-            x_copy(way, rel).wait_send()
+            x_copy(rel, q).wait_send()
 
     def sent(o, u):
-        for loc, all_, rs_, ag_ in (
-            (s_loc, s_all, s_rs_s, s_ag_s),
-            (g_loc, g_all, g_rs_s, g_ag_s),
-        ):
-            part = loc.at[pl.ds(0, PIECE)]
-            remote(part, part, rs_.at[o], rs_.at[o], (d, (s + o) % SEQ)).wait_send()
-            remote(all_.at[s], all_.at[s], ag_.at[o], ag_.at[o], (d, (s + o) % SEQ)).wait_send()
+        for i in range(2):
+            for sums in (s_sums, g_sums):
+                rs_copy(i, sums, o).wait_send()
+                ag_copy(i, sums, o, s).wait_send()
         return u
 
     lax.fori_loop(1, SEQ, sent, 0)
@@ -475,10 +528,10 @@
             V((5 * HEAD + 32, 2 * ROWS), F32), V((5 * HEAD + 32, 256), F32),
             V((2, 5 * HEAD, ROWS), BF), V((5 * HEAD, ROWS), BF), V((2, 5 * HEAD, PAD), F32),
             *summed, *summed,
-            V((PIECE, PAD), F32), V((1, PAD), F32), V((DP, 1, PAD), F32), V((1, PAD), F32), V((SEQ, 1, PAD), F32),
+            V((DP, 1, PAD), F32), V((DP, 1, PAD), F32), V((1, PAD), F32), V((SEQ, 1, PAD), F32),
             dma((4,)), dma((HEADS,)), dma((3,)), dma((3,)), dma((2,)), dma((2,)),
-            dma((2, 4)), dma((2, 4)), dma((2, 7)), dma((2, 7)),
-            *[dma((SEQ,))] * 8,
+            dma((2, 4, PARTS)), dma((2, 4, PARTS)), dma((7, PARTS)), dma((7, PARTS)),
+            *[dma((2, SEQ))] * 8,
             dma((DP,)), dma((DP,)), dma((SEQ,)), dma((SEQ,)),
         ],
         compiler_params=pltpu.CompilerParams(

time: 86.4 us -> 78.6 us (0.910)
  Pallas kernels: 80.9 us -> 73.1 us
    pallas_call x1, Pallas kernels: 80.9 us -> 73.1 us  [local(): pl.pallas_call(kernel, out_shape=(wide, wide, wide, slim, slim), in_specs...]
where the time goes in v3:
time: 78.6 us; the launch traced here: 78.5 us
  Pallas kernels  73.1 us (93%)
  local copies, waits for them, and re-layouts  4.65 us (6%)
    pallas_call x1, Pallas kernels, local(): pl.pallas_call(kernel, out_shape=(wide, wide, wide, slim, slim), in_specs...  73.1 us
    unnamed x13, local copies, waits for them, and re-layouts  4.65 us

profile of v3, /device:TPU:1, one launch (start us, length us, event | category | flops | bytes accessed | tf_op | source)
XLA Modules:
  0.0 78.5 jit_solution(18184441412785363156)
XLA Ops:
  0.6 73.1 %attention_backward.1 = (bf16[1120,256]{1,0:T(8,128)(2,1)}, bf16[1120,256]{1,0:T(8,128)(2,1)}, bf16[1120,256]{1,0:T(8,128)(2,1)}, f32[1,35]{1,0:T(1,128)}, f32[1,35]{1,0:T(1,128)}) custom-call(bf16[2240,256]{1,0:T(8,128)(2,1)} %bitcast.28, bf16[35,2240]{1,0:T(8,128)(2,1)} %w_in.1, bf16[1120,256]{1,0:T(8,128)(2,1)} %bitcast.29, bf16[1120,256]{1,0:T(8,128)(2,1)} %bitcast.30, ...), custom_call_target="tpu_custom_call" | custom-call | flops 1509949440 | bytes 5000000 | tf_op jit(solution)/shard_map/attention_backward/pallas_call | solution.py:518
  73.8 0.0 copy-start.1
  73.8 0.0 copy-start
  73.8 2.0 %copy.17 = bf16[1,256,1120]{1,2,0:T(8,128)(2,1)} copy(bf16[1,256,1120]{1,2,0:T(8,128)(2,1)} %bitcast.27) | data formatting | bytes 1146880
  75.8 0.0 copy-done.1
  75.8 0.0 copy-start.3
  75.8 0.0 copy-start.2
  75.8 0.8 %copy.18 = bf16[1,256,1120]{1,2,0:T(8,128)(2,1)} copy(bf16[1,256,1120]{1,2,0:T(8,128)(2,1)S(1)} %bitcast.26) | data formatting | bytes 1146880
  76.6 0.0 copy-done
  76.6 0.8 %copy.19 = bf16[1,256,1120]{1,2,0:T(8,128)(2,1)} copy(bf16[1,256,1120]{1,2,0:T(8,128)(2,1)S(1)} %bitcast.25) | data formatting | bytes 1146880
  77.4 0.0 copy-done.3
  77.4 0.5 copy.20
  78.0 0.0 copy-done.2
  78.0 0.5 copy.21
Async XLA Ops:
  73.8 2.0 %copy-start.1 = (bf16[1120,256]{1,0:T(8,128)(2,1)S(1)}, bf16[1120,256]{1,0:T(8,128)(2,1)}, u32[]{:S(2)}) copy-start(bf16[1120,256]{1,0:T(8,128)(2,1)} %get-tuple-element.11) | copy-start | bytes 1720324
  73.8 2.8 %copy-start = (bf16[1120,256]{1,0:T(8,128)(2,1)S(1)}, bf16[1120,256]{1,0:T(8,128)(2,1)}, u32[]{:S(2)}) copy-start(bf16[1120,256]{1,0:T(8,128)(2,1)} %get-tuple-element.12) | copy-start | bytes 1720324
  75.8 1.6 %copy-start.3 = (f32[1,35]{1,0:T(1,128)S(1)}, f32[1,35]{1,0:T(1,128)}, u32[]{:S(2)}) copy-start(f32[1,35]{1,0:T(1,128)} %get-tuple-element.13) | copy-start | bytes 424
  75.8 2.1 %copy-start.2 = (f32[1,35]{1,0:T(1,128)S(1)}, f32[1,35]{1,0:T(1,128)}, u32[]{:S(2)}) copy-start(f32[1,35]{1,0:T(1,128)} %get-tuple-element.14) | copy-start | bytes 424

commit v4 on v3

--- a/solution.py
+++ b/solution.py
@@ -22,7 +22,7 @@
 PARTS = HALF // CUT
 WIN = 80
 PIECE = 80
-GROUPS = ((0, 42, 3, 0), (672, 28, 2, 48))
+GROUPS = ((4, 28, 2, 0), (6, 42, 3, 32))
 BF = jnp.bfloat16
 F32 = jnp.float32
 MESH = pl.DeviceIdType.MESH
@@ -55,13 +55,13 @@
 
 def kernel(
     og_in, w_in, q_in, k_in, v_in, gq_in, gk_in,
-    qg_out, kg_out, vg_out, gqg_out, gkg_out,
-    k_raw, q_raw, vx, w_raw, og, rk, rq, ngx,
-    wpk, pair, wbuf, acc, gacc, att, att_send, gqk,
+    qg_out, kg_out, vg_out, total_out,
+    gq_raw, gk_raw, qg, kg, vg, k_raw, q_raw, vx, w_raw, og, rk, rq, ngx,
+    pair, wbuf, acc, gacc, att, att_send, gqk,
     s_loc, s_recv, s_all, s_full,
     g_loc, g_recv, g_all, g_full,
     win_send, win_recv, part_send, part_recv,
-    in_sem, v_sem, misc_s, misc_r, pair_s, pair_r, z_s, z_r, x_s, x_r,
+    in_sem, out_sem, v_sem, misc_s, misc_r, pair_s, pair_r, z_s, z_r, x_s, x_r,
     s_rs_s, s_rs_r, s_ag_s, s_ag_r, g_rs_s, g_rs_r, g_ag_s, g_ag_r, r_s, r_r, t_s, t_r,
 ):
     d = lax.axis_index("dp")
@@ -85,26 +85,40 @@
         )
 
     def head(h):
-        return pl.ds(HEAD * h, HEAD)
+        row = HEAD * h
+        return pl.ds(row if isinstance(row, int) else pl.multiple_of(row, 16), HEAD)
+
+    bases = (6 * c, 4 * (1 - c))
+
+    def heads_of(i):
+        return [bases[i] + n for n in range(GROUPS[i][0])]
+
+    def rows_of(i, first, n):
+        return pl.ds(pl.multiple_of(HEAD * bases[i] + first, 16), n)
 
     mine = pl.ds(0, ROWS)
     theirs = pl.ds(ROWS, ROWS)
     ins = [
         pltpu.make_async_copy(a, b, in_sem.at[i])
         for i, (a, b) in enumerate(
-            ((w_in, w_raw), (k_in, k_raw), (q_in, q_raw), (og_in, og.at[pl.ds(0, MODEL), mine]))
+            (
+                (k_in, k_raw), (q_in, q_raw), (og_in, og.at[pl.ds(0, MODEL), mine]),
+                (w_in, w_raw.at[c]), (gq_in, gq_raw.at[c]), (gk_in, gk_raw.at[c]),
+            )
         )
     ]
     ins_v = [
         pltpu.make_async_copy(v_in.at[head(h)], vx.at[h, pl.ds(0, HEAD)], v_sem.at[h])
         for h in range(HEADS)
     ]
-    ins[0].start()
-    ins[1].start()
-    for cp in ins_v:
+    for cp in (ins[0], *ins_v, ins[1], ins[2]):
         cp.start()
-    ins[2].start()
-    ins[3].start()
+
+    @pl.when(c == y)
+    def _():
+        for cp in ins[3:]:
+            cp.start()
+
     bar = pltpu.get_barrier_semaphore()
 
     def greet_seq(o, u):
@@ -124,21 +138,6 @@
         greet((far_dp, far_seq))
         greet((far_dp + 1, far_seq))
 
-    ins[0].wait()
-    wpk[...] = jnp.zeros_like(wpk)
-    wpk[0:OWN, 0:MODEL] = w_raw[...]
-    diag = iota((48, OWN), 0) == iota((48, OWN), 1)
-    lane = iota((48, 64), 1)
-    extra = jnp.zeros((48, 64), F32)
-    for n, ref in enumerate((gq_in, gk_in)):
-        col = jnp.sum(jnp.where(diag, jnp.broadcast_to(ref[...], (48, OWN)), 0.0), axis=1, keepdims=True)
-        rest = col
-        for m in range(3):
-            part = rest.astype(BF).astype(F32)
-            extra = jnp.where(lane == 3 * n + m, part, extra)
-            rest = rest - part
-    wpk[:, MODEL:] = extra.astype(BF)
-
     ones = jnp.where(iota((16, ROWS), 0) == 0, 1.0, 0.0).astype(BF)
     og[MODEL:, :] = jnp.zeros((2 * HALF - MODEL, 2 * ROWS), BF)
     acc[...] = jnp.zeros_like(acc)
@@ -150,29 +149,38 @@
     def piece_rows(g):
         return pl.ds(g[3], 16 * g[2])
 
-    def rs_copy(i, sums, o):
+    def rs_copy(i, sums, o, n):
+        j = (s + o) % SEQ
+        rows = rows_of(i, first_tile(GROUPS[i], j) * 16, 16 * n)
+        piece = sums[1].at[o, pl.ds(GROUPS[i][3], 16 * n)]
+        return remote(sums[0].at[rows], piece, sums[4].at[i, o], sums[5].at[i, o], (d, j))
+
+    def ag_copy(i, sums, o, j, n):
+        piece = sums[2].at[j, pl.ds(GROUPS[i][3], 16 * n)]
+        return remote(piece, piece, sums[6].at[i, o], sums[7].at[i, o], (d, (s + o) % SEQ))
+
+    def sized(i, j, act):
         g = GROUPS[i]
-        j = (s + o) % SEQ
-        rows = pl.ds(pl.multiple_of(g[0] + first_tile(g, j) * 16, 16), 16 * g[2])
-        return remote(sums[0].at[rows], sums[1].at[o, piece_rows(g)], sums[4].at[i, o], sums[5].at[i, o], (d, j))
-
-    def ag_copy(i, sums, o, j):
-        piece = sums[2].at[j, piece_rows(GROUPS[i])]
-        return remote(piece, piece, sums[6].at[i, o], sums[7].at[i, o], (d, (s + o) % SEQ))
+        owned = first_tile(g, j + 1) - first_tile(g, j)
+        for n in (g[2] - 1, g[2]):
+            pl.when(owned == n)(functools.partial(act, n))
+
+    def each_peer(step):
+        def body(o, u):
+            step(o)
+            return u
+
+        lax.fori_loop(1, SEQ, body, 0)
 
     def rs_send(i, sums):
-        def step(o, u):
-            rs_copy(i, sums, o).start()
-            return u
-
-        lax.fori_loop(1, SEQ, step, 0)
+        each_peer(lambda o: sized(i, (s + o) % SEQ, lambda n: rs_copy(i, sums, o, n).start()))
 
     def rs_sum(i, sums):
         g = GROUPS[i]
-        rows = pl.ds(pl.multiple_of(g[0] + first_tile(g, s) * 16, 16), 16 * g[2])
+        rows = rows_of(i, first_tile(g, s) * 16, 16 * g[2])
 
         def step(o, total):
-            rs_copy(i, sums, o).wait_recv()
+            sized(i, s, lambda n: rs_copy(i, sums, o, n).wait_recv())
             return total + sums[1][o, g[3] : g[3] + 16 * g[2], :].astype(F32)
 
         return lax.fori_loop(1, SEQ, step, sums[0][rows, :].astype(F32))
@@ -180,31 +188,25 @@
     def ag_send(i, sums, total):
         g = GROUPS[i]
         sums[2][s, g[3] : g[3] + 16 * g[2], :] = total.astype(BF)
-
-        def step(o, u):
-            ag_copy(i, sums, o, s).start()
-            return u
-
-        lax.fori_loop(1, SEQ, step, 0)
+        each_peer(lambda o: sized(i, s, lambda n: ag_copy(i, sums, o, s, n).start()))
 
     def ag_wait(i, sums):
         g = GROUPS[i]
 
-        def step(o, u):
-            ag_copy(i, sums, o, (s + SEQ - o) % SEQ).wait_recv()
-            return u
-
-        lax.fori_loop(1, SEQ, step, 0)
+        def step(o):
+            j = (s + SEQ - o) % SEQ
+            sized(i, j, lambda n: ag_copy(i, sums, o, j, n).wait_recv())
+
+        each_peer(step)
         for j in range(SEQ):
-            row = g[0] + 16 * first_tile(g, j)
             n = 16 * OWNER[i].count(j)
-            sums[3][row : row + n, :] = sums[2][j, g[3] : g[3] + n, :]
+            sums[3][rows_of(i, 16 * first_tile(g, j), n), :] = sums[2][j, g[3] : g[3] + n, :]
 
     s_sums = (s_loc, s_recv, s_all, s_full, s_rs_s, s_rs_r, s_ag_s, s_ag_r)
     g_sums = (g_loc, g_recv, g_all, g_full, g_rs_s, g_rs_r, g_ag_s, g_ag_r)
 
     def summary():
-        ins[1].wait()
+        ins[0].wait()
         for h in range(HEADS):
             ins_v[h].wait()
         vx[:, HEAD:, :] = jnp.broadcast_to(ones, (HEADS, PAD - HEAD, ROWS))
@@ -223,17 +225,21 @@
 
     pl.semaphore_wait(bar, SEQ - 1 + 4)
 
-    far = remote(wpk, pair.at[c], pair_s.at[0], pair_r.at[c], (far_dp + y, far_seq))
-    near = remote(wpk, pair.at[c], pair_s.at[1], pair_r.at[c], sib)
-    far.start()
+    def row_copies(kind, dev):
+        return [
+            remote(a, b.at[c], pair_s.at[kind, n], pair_r.at[c, n], dev)
+            for n, (a, b) in enumerate(((w_in, w_raw), (gq_in, gq_raw), (gk_in, gk_raw)))
+        ]
+
+    far = row_copies(0, (far_dp + y, far_seq))
+    near = row_copies(1, sib)
+    for cp in far:
+        cp.start()
 
     @pl.when(c != y)
     def _():
-        near.start()
-
-    @pl.when(c == y)
-    def _():
-        pair[c] = wpk[...]
+        for cp in near:
+            cp.start()
 
     og_copy = remote(og_in, og.at[pl.ds(0, MODEL), theirs], misc_s.at[0], misc_r.at[0], sib)
     og_copy.start()
@@ -243,16 +249,36 @@
         rs_send(0, s_sums)
         rs_send(1, s_sums)
 
-    pair_wait = [remote(wpk, pair.at[i], pair_s.at[0], pair_r.at[i], sib) for i in range(2)]
-
-    @pl.when((c != y) | (c == 1))
-    def _():
-        pair_wait[0].wait_recv()
-
-    @pl.when((c != y) | (c == 0))
-    def _():
-        pair_wait[1].wait_recv()
-
+    def wait_rows(i):
+        for n, (a, b) in enumerate(((w_in, w_raw), (gq_in, gq_raw), (gk_in, gk_raw))):
+            remote(a, b.at[i], pair_s.at[0, n], pair_r.at[i, n], sib).wait_recv()
+
+    wait_rows(1 - c)
+
+    @pl.when(c != y)
+    def _():
+        wait_rows(c)
+
+    @pl.when(c == y)
+    def _():
+        for cp in ins[3:]:
+            cp.wait()
+
+    pair[...] = jnp.zeros_like(pair)
+    diag = iota((48, OWN), 0) == iota((48, OWN), 1)
+    lane = iota((48, 64), 1)
+    for i in range(2):
+        pair[i, 0:OWN, 0:MODEL] = w_raw[i]
+        extra = jnp.zeros((48, 64), F32)
+        for n, ref in enumerate((gq_raw, gk_raw)):
+            rest = jnp.sum(
+                jnp.where(diag, jnp.broadcast_to(ref[i], (48, OWN)), 0.0), axis=1, keepdims=True
+            )
+            for k in range(3):
+                bits = rest.astype(BF).astype(F32)
+                extra = jnp.where(lane == 3 * n + k, bits, extra)
+                rest = rest - bits
+        pair[i, :, MODEL:] = extra.astype(BF)
     m = iota((WIN, 96), 1)
     to = (70 * z) % 16 + jnp.where(m < 48, m, m - 13)
     to = jnp.where(to >= WIN, to - WIN, to)
@@ -321,7 +347,7 @@
         spread = jnp.where(pick & (e == 1), 1.0, 0.0).astype(BF)
         add_rows(gacc, b, dot_nn(wbuf[e, b, :, HALF - 128 :], spread))
 
-    ins[2].wait()
+    ins[1].wait()
     for h in range(HEADS):
         rq[h] = inverse(q_raw[head(h), :].astype(F32))
 
@@ -340,7 +366,7 @@
     def _():
         spread_summary()
 
-    ins[3].wait()
+    ins[2].wait()
     og_copy.wait_recv()
     product(p, z)
     product(1 - p, z)
@@ -360,17 +386,17 @@
 
     half_heads = 5 * HEAD
     att_send[...] = acc[0:half_heads, ROWS:].astype(BF)
-    att_copy = remote(att_send, att.at[c], misc_s.at[2], misc_r.at[2], sib)
+    own_rows = pl.ds(pl.multiple_of(half_heads * c, 16), half_heads)
+    other_rows = pl.ds(pl.multiple_of(half_heads * (1 - c), 16), half_heads)
+    att_copy = remote(att_send, att.at[own_rows], misc_s.at[2], misc_r.at[2], sib)
     att_copy.start()
-    gqk[c] = gacc[0:half_heads, 0:128] * gacc[0:half_heads, 128:]
-    gain_copy = remote(gqk.at[c], gqk.at[c], misc_s.at[1], misc_r.at[1], sib)
+    gqk[own_rows, :] = gacc[0:half_heads, 0:128] * gacc[0:half_heads, 128:]
+    gain_copy = remote(gqk.at[own_rows], gqk.at[own_rows], misc_s.at[1], misc_r.at[1], sib)
     gain_copy.start()
-    att[c] = acc[0:half_heads, 0:ROWS].astype(BF)
-    remote(gqk.at[1 - c], gqk.at[1 - c], misc_s.at[1], misc_r.at[1], sib).wait_recv()
-    remote(att_send, att.at[1 - c], misc_s.at[2], misc_r.at[2], sib).wait_recv()
+    att[own_rows, :] = acc[0:half_heads, 0:ROWS].astype(BF)
 
     def gain(h):
-        g = gqk[h // 5, HEAD * (h % 5) : HEAD * (h % 5 + 1), :]
+        g = gqk[head(h), :]
         return jnp.concatenate([g, g], axis=1)
 
     first = iota((16, ROWS), 0) == 0
@@ -378,7 +404,7 @@
         phi = jnp.maximum(q_raw[head(h), :].astype(F32) * rq[h], 0.0)
         num = dot_tn(s_full[head(h), :], (phi * gain(h)).astype(BF))
         inv = 1.0 / (num[HEAD : HEAD + 1] + float(TOKENS))
-        ng = att[h // 5, HEAD * (h % 5) : HEAD * (h % 5 + 1), :].astype(F32) * inv
+        ng = att[head(h), :].astype(F32) * inv
         dg = -jnp.sum(ng * num[0:HEAD], axis=0, keepdims=True) * inv
         ngx[h, 0:HEAD, :] = ng.astype(BF)
         ngx[h, HEAD:, :] = jnp.where(first, dg, 0.0).astype(BF)
@@ -395,10 +421,12 @@
         return dot_nn(which, hi) + dot_nn(which, lo)
 
     wins = jnp.zeros((DP, PAD), F32)
-    for h in range(0, 6):
+    for h in heads_of(0):
         wins = wins + grads_of(h)
     rs_send(0, g_sums)
-    for h in range(6, HEADS):
+    remote(gqk.at[other_rows], gqk.at[other_rows], misc_s.at[1], misc_r.at[1], sib).wait_recv()
+    remote(att_send, att.at[other_rows], misc_s.at[2], misc_r.at[2], sib).wait_recv()
+    for h in heads_of(1):
         wins = wins + grads_of(h)
     rs_send(1, g_sums)
     win_send[...] = wins.reshape(DP, 1, PAD)
@@ -422,10 +450,12 @@
 
     def query_grad(h):
         g = dot_nn(s_full[head(h), :], ngx[h]) * gain(h)
-        qg_out[head(h), :] = norm_back(q_raw[head(h), :], rq[h], g)
+        qg[head(h), :] = norm_back(q_raw[head(h), :], rq[h], g)
 
     for h in range(HEADS):
         query_grad(h)
+    outs = [pltpu.make_async_copy(qg, qg_out, out_sem.at[0])]
+    outs[0].start()
 
     for i in range(2):
         ag_send(i, g_sums, rs_sum(i, g_sums))
@@ -448,30 +478,35 @@
         gg = gain(h)
         kf = k_raw[head(h), :].astype(F32)
         g = dot_nn(g_full[head(h), :], vx[h]) * gg
-        kg_out[head(h), :] = norm_back(k_raw[head(h), :], rk[h], g)
+        kg[head(h), :] = norm_back(k_raw[head(h), :], rk[h], g)
         phi = (jnp.maximum(kf * rk[h], 0.0) * gg).astype(BF)
-        vg_out[head(h), :] = dot_tn(g_full[head(h), :], phi)[0:HEAD].astype(BF)
-
-    ag_wait(0, g_sums)
-    for h in range(0, 6):
-        key_grad(h)
-    ag_wait(1, g_sums)
-    for h in range(6, HEADS):
-        key_grad(h)
+        vg[head(h), :] = dot_tn(g_full[head(h), :], phi)[0:HEAD].astype(BF)
+
+    for i in range(2):
+        ag_wait(i, g_sums)
+        for h in heads_of(i):
+            key_grad(h)
+        rows = rows_of(i, 0, HEAD * GROUPS[i][0])
+        for n, (a, b) in enumerate(((kg, kg_out), (vg, vg_out))):
+            outs.append(pltpu.make_async_copy(a.at[rows], b.at[rows], out_sem.at[1 + 2 * i + n]))
+            outs[-1].start()
 
     def part_sum(o, total):
         part_copy(o).wait_recv()
         return total + part_recv[o]
 
     total = lax.fori_loop(1, SEQ, part_sum, part_send[...])
-    gqg_out[...] = total[:, 0:OWN] * gk_in[...]
-    gkg_out[...] = total[:, 0:OWN] * gq_in[...]
-
-    far.wait_send()
+    total_out[...] = total[:, 0:OWN]
+
+    for cp in outs:
+        cp.wait()
+    for cp in far:
+        cp.wait_send()
 
     @pl.when(c != y)
     def _():
-        near.wait_send()
+        for cp in near:
+            cp.wait_send()
 
     og_copy.wait_send()
     gain_copy.wait_send()
@@ -487,8 +522,8 @@
     def sent(o, u):
         for i in range(2):
             for sums in (s_sums, g_sums):
-                rs_copy(i, sums, o).wait_send()
-                ag_copy(i, sums, o, s).wait_send()
+                sized(i, (s + o) % SEQ, lambda n: rs_copy(i, sums, o, n).wait_send())
+                sized(i, s, lambda n: ag_copy(i, sums, o, s, n).wait_send())
         return u
 
     lax.fori_loop(1, SEQ, sent, 0)
@@ -504,6 +539,12 @@
         return u
 
     lax.fori_loop(1, SEQ, part_sent, 0)
+
+
+def hand_over(qg_in, kg_in, vg_in, qg_out, kg_out, vg_out):
+    qg_out[...] = qg_in[...]
+    kg_out[...] = kg_in[...]
+    vg_out[...] = vg_in[...]
 
 
 def local(out_grad, out_weight, queries, keys, values, query_gain, key_norm_gain):
@@ -517,19 +558,19 @@
     ]
     outs = pl.pallas_call(
         kernel,
-        out_shape=(wide, wide, wide, slim, slim),
-        in_specs=[any_] * 5 + [vm] * 2,
-        out_specs=(vm,) * 5,
+        out_shape=(wide, wide, wide, slim),
+        in_specs=[any_] * 7,
+        out_specs=(any_,) * 3 + (vm,),
         scratch_shapes=[
-            V((WIDTH, ROWS), BF), V((WIDTH, ROWS), BF), V((HEADS, PAD, ROWS), BF),
-            V((OWN, MODEL), BF), V((2 * HALF, 2 * ROWS), BF),
+            V((2, 1, OWN), F32), V((2, 1, OWN), F32), *[V((WIDTH, ROWS), BF)] * 5, V((HEADS, PAD, ROWS), BF),
+            V((2, OWN, MODEL), BF), V((2 * HALF, 2 * ROWS), BF),
             V((HEADS, 1, ROWS), F32), V((HEADS, 1, ROWS), F32), V((HEADS, PAD, ROWS), BF),
-            V((48, 2 * HALF), BF), V((2, 48, 2 * HALF), BF), V((2, 8, WIN, HALF), BF),
+            V((2, 48, 2 * HALF), BF), V((2, 8, WIN, HALF), BF),
             V((5 * HEAD + 32, 2 * ROWS), F32), V((5 * HEAD + 32, 256), F32),
-            V((2, 5 * HEAD, ROWS), BF), V((5 * HEAD, ROWS), BF), V((2, 5 * HEAD, PAD), F32),
+            V((WIDTH, ROWS), BF), V((5 * HEAD, ROWS), BF), V((WIDTH, PAD), F32),
             *summed, *summed,
             V((DP, 1, PAD), F32), V((DP, 1, PAD), F32), V((1, PAD), F32), V((SEQ, 1, PAD), F32),
-            dma((4,)), dma((HEADS,)), dma((3,)), dma((3,)), dma((2,)), dma((2,)),
+            dma((6,)), dma((5,)), dma((HEADS,)), dma((3,)), dma((3,)), dma((2, 3)), dma((2, 3)),
             dma((2, 4, PARTS)), dma((2, 4, PARTS)), dma((7, PARTS)), dma((7, PARTS)),
             *[dma((2, SEQ))] * 8,
             dma((DP,)), dma((DP,)), dma((SEQ,)), dma((SEQ,)),
@@ -545,8 +586,18 @@
         out_grad[0].T, out_weight, queries[0].T, keys[0].T, values[0].T,
         query_gain.reshape(1, OWN), key_norm_gain.reshape(1, OWN),
     )
-    qg, kg, vg, gq, gk = outs
-    return qg.T[None], kg.T[None], vg.T[None], gq.reshape(OWN), gk.reshape(OWN)
+    qg, kg, vg, total = outs
+    total = total.reshape(OWN)
+    block = pl.BlockSpec((560, ROWS), lambda i: (i, 0))
+    qg, kg, vg = pl.pallas_call(
+        hand_over,
+        grid=(2,),
+        out_shape=(wide, wide, wide),
+        in_specs=[block] * 3,
+        out_specs=(block,) * 3,
+        name="hand_over",
+    )(qg, kg, vg)
+    return qg.T[None], kg.T[None], vg.T[None], total * key_norm_gain, total * query_gain
 
 
 def solution(mesh):

time: 78.6 us -> 73.7 us (0.938)
  local copies, waits for them, and re-layouts: 4.65 us -> 0.02 us
  Pallas kernels: 73.1 us -> 72.3 us
    unnamed x13 -> x6, local copies, waits for them, and re-layouts: 4.65 us -> 0.02 us
    pallas_call x1 -> x2, Pallas kernels: 73.1 us -> 72.3 us  [the longest x1 69.9 us: local(): pl.pallas_call(kernel, out_shape=(wide, wide, wide, slim), in_specs=[any_...]
where the time goes in v4:
time: 73.7 us; the launch traced here: 73.5 us
  Pallas kernels  72.3 us (98%)
    pallas_call x1, Pallas kernels, local(): pl.pallas_call(kernel, out_shape=(wide, wide, wide, slim), in_specs=[any_...  69.9 us
    pallas_call x1, Pallas kernels, local(): pl.pallas_call(hand_over, grid=(2,), out_shape=(wide, wide, wide), in_spe...  2.39 us

profile of v4, /device:TPU:1, one launch (start us, length us, event | category | flops | bytes accessed | tf_op | source)
XLA Modules:
  0.0 73.5 jit_solution(4797886655280009448)
XLA Ops:
  0.6 69.9 %attention_backward.1 = (bf16[1120,256]{1,0:T(8,128)(2,1)}, bf16[1120,256]{1,0:T(8,128)(2,1)}, bf16[1120,256]{1,0:T(8,128)(2,1)}, f32[1,35]{1,0:T(1,128)}) custom-call(bf16[2240,256]{1,0:T(8,128)(2,1)} %bitcast.28, bf16[35,2240]{1,0:T(8,128)(2,1)} %w_in.1, bf16[1120,256]{1,0:T(8,128)(2,1)} %bitcast.29, bf16[1120,256]{1,0:T(8,128)(2,1)} %bitcast.30, ...), custom_call_target="tpu_custom_call" | custom-call | flops 1509949440 | bytes 5000000 | tf_op jit(solution)/shard_map/attention_backward/pallas_call | solution.py:559
  70.6 0.0 copy-start
  70.6 0.0 copy-start.1
  70.6 0.0 copy-start.2
  70.6 2.4 %hand_over.1 = (bf16[1120,256]{1,0:T(8,128)(2,1)}, bf16[1120,256]{1,0:T(8,128)(2,1)}, bf16[1120,256]{1,0:T(8,128)(2,1)}) custom-call(bf16[1120,256]{1,0:T(8,128)(2,1)} %get-tuple-element.12.qg_in, bf16[1120,256]{1,0:T(8,128)(2,1)} %get-tuple-element.13.kg_in, bf16[1120,256]{1,0:T(8,128)(2,1)} %get-tuple-element.14.vg_in), custom_call_target="tpu_custom_call" | custom-call | tf_op jit(solution)/shard_map/hand_over/pallas_call | solution.py:592
  73.0 0.0 copy-done
  73.0 0.0 copy-done.1
  73.0 0.0 copy-done.2
  73.0 0.5 bitcast_multiply_fusion
Async XLA Ops:
  70.6 2.4 %copy-start = (f32[35]{0:T(128)S(1)}, f32[35]{0:T(128)}, u32[]{:S(2)}) copy-start(f32[35]{0:T(128)} %param.12) | copy-start | bytes 424
  70.6 2.4 %copy-start.1 = (f32[35]{0:T(128)S(1)}, f32[35]{0:T(128)}, u32[]{:S(2)}) copy-start(f32[35]{0:T(128)} %param.13) | copy-start | bytes 424
  70.6 2.4 %copy-start.2 = (f32[1,35]{1,0:T(1,128)S(1)}, f32[1,35]{1,0:T(1,128)}, u32[]{:S(2)}) copy-start(f32[1,35]{1,0:T(1,128)} %get-tuple-element.18) | copy-start | bytes 424

commit v5 on v4

--- a/solution.py
+++ b/solution.py
@@ -225,20 +225,29 @@
 
     pl.semaphore_wait(bar, SEQ - 1 + 4)
 
-    def row_copies(kind, dev):
+    def row_copy(kind, i, dev, e=None):
+        cols = pl.ds(0, MODEL) if e is None else pl.ds(HALF * e, (HALF, MODEL - HALF)[e])
+        src, dst = (w_in, w_raw.at[i]) if e is None else (w_in.at[:, cols], w_raw.at[i, :, cols])
+        return remote(src, dst, pair_s.at[kind, 0], pair_r.at[i, 0], dev)
+
+    def gain_copies(kind, i, dev):
         return [
-            remote(a, b.at[c], pair_s.at[kind, n], pair_r.at[c, n], dev)
-            for n, (a, b) in enumerate(((w_in, w_raw), (gq_in, gq_raw), (gk_in, gk_raw)))
+            remote(a, b.at[i], pair_s.at[kind, n], pair_r.at[i, n], dev)
+            for n, a, b in ((1, gq_in, gq_raw), (2, gk_in, gk_raw))
         ]
 
-    far = row_copies(0, (far_dp + y, far_seq))
-    near = row_copies(1, sib)
-    for cp in far:
+    def by_half(act):
+        for e in range(2):
+            pl.when(p == e)(functools.partial(act, e))
+
+    far_dev = (far_dp + y, far_seq)
+    by_half(lambda e: row_copy(0, c, far_dev, e).start())
+    for cp in gain_copies(0, c, far_dev):
         cp.start()
 
     @pl.when(c != y)
     def _():
-        for cp in near:
+        for cp in (row_copy(1, c, sib), *gain_copies(1, c, sib)):
             cp.start()
 
     og_copy = remote(og_in, og.at[pl.ds(0, MODEL), theirs], misc_s.at[0], misc_r.at[0], sib)
@@ -249,18 +258,17 @@
         rs_send(0, s_sums)
         rs_send(1, s_sums)
 
-    def wait_rows(i):
-        for n, (a, b) in enumerate(((w_in, w_raw), (gq_in, gq_raw), (gk_in, gk_raw))):
-            remote(a, b.at[i], pair_s.at[0, n], pair_r.at[i, n], sib).wait_recv()
-
-    wait_rows(1 - c)
-
     @pl.when(c != y)
     def _():
-        wait_rows(c)
+        for i in range(2):
+            by_half(lambda e: row_copy(0, i, sib, e).wait_recv())
+            for cp in gain_copies(0, i, sib):
+                cp.wait_recv()
 
     @pl.when(c == y)
     def _():
+        for cp in (row_copy(0, 1 - c, sib), *gain_copies(0, 1 - c, sib)):
+            cp.wait_recv()
         for cp in ins[3:]:
             cp.wait()
 
@@ -286,8 +294,11 @@
     place = jnp.where((iota((WIN, 96), 0) == to) & good, 1.0, 0.0).astype(BF)
     both = pair[...].reshape(96, 2 * HALF)
     window = dot_nn(place, both).astype(BF)
-    wbuf[0, z] = window[:, :HALF]
-    wbuf[1, z] = window[:, HALF:]
+    for e in range(2):
+
+        @pl.when((p == e) | (c == y))
+        def _():
+            wbuf[e, z] = window[:, HALF * e : HALF * (e + 1)]
 
     def part(e, b, q):
         return wbuf.at[e, b, :, pl.ds(CUT * q, CUT)]
@@ -299,12 +310,12 @@
 
     def x_copy(rel, q):
         ref = part(p, (z + rel) % 8, q)
-        return remote(ref, ref, x_s.at[rel - 1, q], x_r.at[rel - 1, q], right if (q + rel) % 2 == 0 else left)
+        return remote(ref, ref, x_s.at[rel, q], x_r.at[rel, q], right if (q + rel) % 2 == 0 else left)
 
     def x_wait(rel):
         for q in range(PARTS):
             ref = part(1 - p, (z + rel) % 8, q)
-            remote(ref, ref, x_s.at[rel - 1, q], x_r.at[rel - 1, q], right).wait_recv()
+            remote(ref, ref, x_s.at[rel, q], x_r.at[rel, q], right).wait_recv()
 
     def goes(way, k, q):
         return k < 4 or q % 2 == way
@@ -322,6 +333,11 @@
         z_copy(0, 1, q).start()
         z_copy(1, 1, q).start()
 
+    @pl.when(c != y)
+    def _():
+        for q in range(PARTS):
+            x_copy(0, q).start()
+
     @pl.when(z >= 4)
     def _():
         summary()
@@ -369,13 +385,17 @@
     ins[2].wait()
     og_copy.wait_recv()
     product(p, z)
-    product(1 - p, z)
     z_step(3)
     for rel in (1, 7, 2, 6):
         product(p, (z + rel) % 8)
     z_step(4)
     ag_wait(0, s_sums)
     ag_wait(1, s_sums)
+    @pl.when(c != y)
+    def _():
+        x_wait(0)
+
+    product(1 - p, z)
     for rel in (1, 7, 2, 6):
         x_wait(rel)
         product(1 - p, (z + rel) % 8)
@@ -500,13 +520,16 @@
 
     for cp in outs:
         cp.wait()
-    for cp in far:
+    by_half(lambda e: row_copy(0, c, far_dev, e).wait_send())
+    for cp in gain_copies(0, c, far_dev):
         cp.wait_send()
 
     @pl.when(c != y)
     def _():
-        for cp in near:
+        for cp in (row_copy(1, c, sib), *gain_copies(1, c, sib)):
             cp.wait_send()
+        for q in range(PARTS):
+            x_copy(0, q).wait_send()
 
     og_copy.wait_send()
     gain_copy.wait_send()
@@ -571,7 +594,7 @@
             *summed, *summed,
             V((DP, 1, PAD), F32), V((DP, 1, PAD), F32), V((1, PAD), F32), V((SEQ, 1, PAD), F32),
             dma((6,)), dma((5,)), dma((HEADS,)), dma((3,)), dma((3,)), dma((2, 3)), dma((2, 3)),
-            dma((2, 4, PARTS)), dma((2, 4, PARTS)), dma((7, PARTS)), dma((7, PARTS)),
+            dma((2, 4, PARTS)), dma((2, 4, PARTS)), dma((8, PARTS)), dma((8, PARTS)),
             *[dma((2, SEQ))] * 8,
             dma((DP,)), dma((DP,)), dma((SEQ,)), dma((SEQ,)),
         ],

time: 73.7 us -> 70.9 us (0.962)
  Pallas kernels: 72.3 us -> 69.5 us
    pallas_call x1, Pallas kernels: 69.9 us -> 67.1 us  [local(): pl.pallas_call(kernel, out_shape=(wide, wide, wide, slim), in_specs=[any_...]
where the time goes in v5:
time: 70.9 us; the launch traced here: 70.7 us
  Pallas kernels  69.5 us (98%)
    pallas_call x1, Pallas kernels, local(): pl.pallas_call(kernel, out_shape=(wide, wide, wide, slim), in_specs=[any_...  67.1 us
    pallas_call x1, Pallas kernels, local(): pl.pallas_call(hand_over, grid=(2,), out_shape=(wide, wide, wide), in_spe...  2.39 us

profile of v5, /device:TPU:1, one launch (start us, length us, event | category | flops | bytes accessed | tf_op | source)
XLA Modules:
  0.0 70.7 jit_solution(3750239592373564091)
XLA Ops:
  0.6 67.1 %attention_backward.1 = (bf16[1120,256]{1,0:T(8,128)(2,1)}, bf16[1120,256]{1,0:T(8,128)(2,1)}, bf16[1120,256]{1,0:T(8,128)(2,1)}, f32[1,35]{1,0:T(1,128)}) custom-call(bf16[2240,256]{1,0:T(8,128)(2,1)} %bitcast.28, bf16[35,2240]{1,0:T(8,128)(2,1)} %w_in.1, bf16[1120,256]{1,0:T(8,128)(2,1)} %bitcast.29, bf16[1120,256]{1,0:T(8,128)(2,1)} %bitcast.30, ...), custom_call_target="tpu_custom_call" | custom-call | flops 1509949440 | bytes 5000000 | tf_op jit(solution)/shard_map/attention_backward/pallas_call | solution.py:582
  67.8 0.0 copy-start
  67.8 0.0 copy-start.1
  67.8 0.0 copy-start.2
  67.8 2.4 %hand_over.1 = (bf16[1120,256]{1,0:T(8,128)(2,1)}, bf16[1120,256]{1,0:T(8,128)(2,1)}, bf16[1120,256]{1,0:T(8,128)(2,1)}) custom-call(bf16[1120,256]{1,0:T(8,128)(2,1)} %get-tuple-element.12.qg_in, bf16[1120,256]{1,0:T(8,128)(2,1)} %get-tuple-element.13.kg_in, bf16[1120,256]{1,0:T(8,128)(2,1)} %get-tuple-element.14.vg_in), custom_call_target="tpu_custom_call" | custom-call | tf_op jit(solution)/shard_map/hand_over/pallas_call | solution.py:615
  70.2 0.0 copy-done
  70.2 0.0 copy-done.1
  70.2 0.0 copy-done.2
  70.2 0.5 bitcast_multiply_fusion
Async XLA Ops:
  67.8 2.4 %copy-start = (f32[35]{0:T(128)S(1)}, f32[35]{0:T(128)}, u32[]{:S(2)}) copy-start(f32[35]{0:T(128)} %param.12) | copy-start | bytes 424
  67.8 2.4 %copy-start.1 = (f32[35]{0:T(128)S(1)}, f32[35]{0:T(128)}, u32[]{:S(2)}) copy-start(f32[35]{0:T(128)} %param.13) | copy-start | bytes 424
  67.8 2.4 %copy-start.2 = (f32[1,35]{1,0:T(1,128)S(1)}, f32[1,35]{1,0:T(1,128)}, u32[]{:S(2)}) copy-start(f32[1,35]{1,0:T(1,128)} %get-tuple-element.18) | copy-start | bytes 424

commit v6 on v5

--- a/solution.py
+++ b/solution.py
@@ -60,7 +60,7 @@
     pair, wbuf, acc, gacc, att, att_send, gqk,
     s_loc, s_recv, s_all, s_full,
     g_loc, g_recv, g_all, g_full,
-    win_send, win_recv, part_send, part_recv,
+    g_wide, win_send, win_recv, part_send, part_recv,
     in_sem, out_sem, v_sem, misc_s, misc_r, pair_s, pair_r, z_s, z_r, x_s, x_r,
     s_rs_s, s_rs_r, s_ag_s, s_ag_r, g_rs_s, g_rs_r, g_ag_s, g_ag_r, r_s, r_r, t_s, t_r,
 ):
@@ -429,8 +429,11 @@
         ngx[h, 0:HEAD, :] = ng.astype(BF)
         ngx[h, HEAD:, :] = jnp.where(first, dg, 0.0).astype(BF)
         local = dot_nt(phi.astype(BF), ngx[h])
+        g_wide[head(h), :] = local
         g_loc[head(h), :] = local.astype(BF)
-        sums = jnp.sum(local * s_full[head(h), :].astype(F32), axis=1, keepdims=True)
+
+    def windows_of(h):
+        sums = jnp.sum(g_wide[head(h), :] * s_full[head(h), :].astype(F32), axis=1, keepdims=True)
         i_col = HEAD * h + iota((HEAD, PAD), 0)
         spot = i_col - OWN * ((i_col * 1873) >> 16) == iota((HEAD, PAD), 1)
         spread = jnp.where(spot, jnp.broadcast_to(sums, (HEAD, PAD)), 0.0)
@@ -440,15 +443,17 @@
         lo = (spread - hi.astype(F32)).astype(BF)
         return dot_nn(which, hi) + dot_nn(which, lo)
 
-    wins = jnp.zeros((DP, PAD), F32)
     for h in heads_of(0):
-        wins = wins + grads_of(h)
+        grads_of(h)
     rs_send(0, g_sums)
     remote(gqk.at[other_rows], gqk.at[other_rows], misc_s.at[1], misc_r.at[1], sib).wait_recv()
     remote(att_send, att.at[other_rows], misc_s.at[2], misc_r.at[2], sib).wait_recv()
     for h in heads_of(1):
-        wins = wins + grads_of(h)
+        grads_of(h)
     rs_send(1, g_sums)
+    wins = jnp.zeros((DP, PAD), F32)
+    for h in range(HEADS):
+        wins = wins + windows_of(h)
     win_send[...] = wins.reshape(DP, 1, PAD)
 
     def win_copy(o):
@@ -592,7 +597,7 @@
             V((5 * HEAD + 32, 2 * ROWS), F32), V((5 * HEAD + 32, 256), F32),
             V((WIDTH, ROWS), BF), V((5 * HEAD, ROWS), BF), V((WIDTH, PAD), F32),
             *summed, *summed,
-            V((DP, 1, PAD), F32), V((DP, 1, PAD), F32), V((1, PAD), F32), V((SEQ, 1, PAD), F32),
+            V((WIDTH, PAD), F32), V((DP, 1, PAD), F32), V((DP, 1, PAD), F32), V((1, PAD), F32), V((SEQ, 1, PAD), F32),
             dma((6,)), dma((5,)), dma((HEADS,)), dma((3,)), dma((3,)), dma((2, 3)), dma((2, 3)),
             dma((2, 4, PARTS)), dma((2, 4, PARTS)), dma((8, PARTS)), dma((8, PARTS)),
             *[dma((2, SEQ))] * 8,

time: 70.9 us -> 71 us (level)
  no operation moved by 1% of the time
where the time goes in v6:
time: 71 us; the launch traced here: 70.8 us
  Pallas kernels  69.6 us (98%)
    pallas_call x1, Pallas kernels, local(): pl.pallas_call(kernel, out_shape=(wide, wide, wide, slim), in_specs=[any_...  67.2 us
    pallas_call x1, Pallas kernels, local(): pl.pallas_call(hand_over, grid=(2,), out_shape=(wide, wide, wide), in_spe...  2.39 us

profile of v6, /device:TPU:1, one launch (start us, length us, event | category | flops | bytes accessed | tf_op | source)
XLA Modules:
  0.0 70.8 jit_solution(1617719958537832795)
XLA Ops:
  0.6 67.2 %attention_backward.1 = (bf16[1120,256]{1,0:T(8,128)(2,1)}, bf16[1120,256]{1,0:T(8,128)(2,1)}, bf16[1120,256]{1,0:T(8,128)(2,1)}, f32[1,35]{1,0:T(1,128)}) custom-call(bf16[2240,256]{1,0:T(8,128)(2,1)} %bitcast.28, bf16[35,2240]{1,0:T(8,128)(2,1)} %w_in.1, bf16[1120,256]{1,0:T(8,128)(2,1)} %bitcast.29, bf16[1120,256]{1,0:T(8,128)(2,1)} %bitcast.30, ...), custom_call_target="tpu_custom_call" | custom-call | flops 1509949440 | bytes 5000000 | tf_op jit(solution)/shard_map/attention_backward/pallas_call | solution.py:587
  67.9 0.0 copy-start
  67.9 0.0 copy-start.1
  67.9 0.0 copy-start.2
  67.9 2.4 %hand_over.1 = (bf16[1120,256]{1,0:T(8,128)(2,1)}, bf16[1120,256]{1,0:T(8,128)(2,1)}, bf16[1120,256]{1,0:T(8,128)(2,1)}) custom-call(bf16[1120,256]{1,0:T(8,128)(2,1)} %get-tuple-element.12.qg_in, bf16[1120,256]{1,0:T(8,128)(2,1)} %get-tuple-element.13.kg_in, bf16[1120,256]{1,0:T(8,128)(2,1)} %get-tuple-element.14.vg_in), custom_call_target="tpu_custom_call" | custom-call | tf_op jit(solution)/shard_map/hand_over/pallas_call | solution.py:620
  70.3 0.0 copy-done
  70.3 0.0 copy-done.1
  70.3 0.0 copy-done.2
  70.3 0.5 bitcast_multiply_fusion
Async XLA Ops:
  67.9 2.4 %copy-start = (f32[35]{0:T(128)S(1)}, f32[35]{0:T(128)}, u32[]{:S(2)}) copy-start(f32[35]{0:T(128)} %param.12) | copy-start | bytes 424
  67.9 2.4 %copy-start.1 = (f32[35]{0:T(128)S(1)}, f32[35]{0:T(128)}, u32[]{:S(2)}) copy-start(f32[35]{0:T(128)} %param.13) | copy-start | bytes 424
  67.9 2.4 %copy-start.2 = (f32[1,35]{1,0:T(1,128)S(1)}, f32[1,35]{1,0:T(1,128)}, u32[]{:S(2)}) copy-start(f32[1,35]{1,0:T(1,128)} %get-tuple-element.18) | copy-start | bytes 424
